TPU v7x, 32 devices: a whole 2x2x4 slice. The times are simulated.
32 devices in a mesh: dp: 8 (over y, x, core), seq: 4 (over z).
Axes of the slice: x: 2, y: 2, z: 4, core: 2. Of those that a mesh axis runs over, the one named last changes fastest.
Arguments:
- activations: bfloat16 [16, 1024, 768], P('dp', 'seq'), may hold values from -6 to 6
- cotangent: bfloat16 [16, 1024, 768], P('dp', 'seq'), may hold values from -6 to 6
- segment_ids: int32 [16, 1024], P('dp'), may hold values from 0 to 2, as said below
- inputs_weight: float32 [768, 2304], P('seq'), may hold values from -0.21875 to 0.21875
- inputs_moment: float32 [768, 2304], P('seq')
- inputs_second: float32 [768, 2304], P('seq'), as said below
- output_weight: float32 [768, 768], P('seq'), may hold values from -2.5 to 2.5
- output_moment: float32 [768, 768], P('seq')
- output_second: float32 [768, 768], P('seq'), as said below
- expand_weight: float32 [768, 3072], P('seq'), may hold values from -0.21875 to 0.21875
- expand_moment: float32 [768, 3072], P('seq')
- expand_second: float32 [768, 3072], P('seq'), as said below
- reduce_weight: float32 [3072, 768], P('seq'), may hold values from -0.109375 to 0.109375
- reduce_moment: float32 [3072, 768], P('seq')
- reduce_second: float32 [3072, 768], P('seq'), as said below
- vector_params: float32 [12, 768], P(None, 'seq')
- vector_moment: float32 [12, 768], P(None, 'seq')
- vector_second: float32 [12, 768], P(None, 'seq'), as said below
Outputs:
- layer_output: bfloat16 [16, 1024, 768], P('dp', 'seq')
- input_grad: bfloat16 [16, 1024, 768], P('dp', 'seq')
- renewed_inputs: float32 [768, 2304], P('seq')
- momentum_inputs: float32 [768, 2304], P('seq')
- variance_inputs: float32 [768, 2304], P('seq')
- renewed_output: float32 [768, 768], P('seq')
- momentum_output: float32 [768, 768], P('seq')
- variance_output: float32 [768, 768], P('seq')
- renewed_expand: float32 [768, 3072], P('seq')
- momentum_expand: float32 [768, 3072], P('seq')
- variance_expand: float32 [768, 3072], P('seq')
- renewed_reduce: float32 [3072, 768], P('seq')
- momentum_reduce: float32 [3072, 768], P('seq')
- variance_reduce: float32 [3072, 768], P('seq')
- renewed_vectors: float32 [12, 768], P(None, 'seq')
- momentum_vectors: float32 [12, 768], P(None, 'seq')
- variance_vectors: float32 [12, 768], P(None, 'seq')
Inputs may be any that keep to these rules, and one draw needn't show every extreme that they name: `segment_ids`: in each sequence the segment number is 0 on a first run of positions, 1 on a middle run and 2 on a last run; the first and the last run each hold 204 to 255 positions. `inputs_second`: entries are positive. `output_second`: entries are positive. `expand_second`: entries are positive. `reduce_second`: entries are positive. `vector_second`: entries are positive.
All inputs are finite; a program needn't handle non-finite values.
Results may differ from a plain program's by a relative error of at most 0.014.
Values may be sent and summed in bfloat16 or wider, within the bound.
No kernel may reach another device: no remote copies, remote signals or barrier semaphores. Data moves between devices by JAX's collectives and lax.ppermute only.
A program may use at most 256 MiB of HBM per device.

v0:
```python
from functools import partial

import jax
import jax.numpy as jnp
from jax import lax
from jax.sharding import PartitionSpec as P

HEADS = 12
HD = 64
STEP = 10


eps_norm = 1e-05
eps_adam = 1e-08
beta_one = 0.9
beta_two = 0.95
decay_rate = 0.1
mask_fill = -1e30


def layer_norm(values, norm_gain, norm_shift):
    center = jnp.mean(values, axis=-1, keepdims=True)
    offsets = values - center
    spread = jnp.mean(offsets * offsets, axis=-1, keepdims=True)
    return offsets * lax.rsqrt(spread + eps_norm) * norm_gain + norm_shift


def contract_rows(left_side, right_side):
    return lax.dot_general(
        left_side, right_side, (((0,), (0,)), ((), ())), preferred_element_type=jnp.float32
    )


def contract_cols(left_side, right_side):
    return lax.dot_general(
        left_side, right_side, (((1,), (1,)), ((), ())), preferred_element_type=jnp.float32
    )


def adamw_step(weight, moment, second, gradient, step_rate, weight_decay):
    moment_new = beta_one * moment + (1.0 - beta_one) * gradient
    second_new = beta_two * second + (1.0 - beta_two) * gradient * gradient
    fix_one = 1.0 - beta_one**STEP
    fix_two = 1.0 - beta_two**STEP
    update = moment_new / fix_one / (jnp.sqrt(second_new / fix_two) + eps_adam)
    return (weight - step_rate * (update + weight_decay * weight), moment_new, second_new)


def score_block(query_heads, key_heads, allowed):
    scores = jnp.einsum(
        "qhd,khd->hqk", query_heads, key_heads, preferred_element_type=jnp.float32
    ) * HD ** (-0.5)
    return jnp.where(allowed[None], scores, mask_fill)


def attend_forward(operands):
    queries, keys_all, values_all, allowed = operands
    row_count = queries.shape[0]
    key_count = keys_all.shape[0]
    query_heads = queries.reshape(row_count, HEADS, HD)
    key_heads = keys_all.reshape(key_count, HEADS, HD)
    value_heads = values_all.reshape(key_count, HEADS, HD)
    masked = score_block(query_heads, key_heads, allowed)
    highest = jnp.max(masked, axis=-1, keepdims=True)
    exponent = jnp.exp(masked - highest)
    totals = jnp.sum(exponent, axis=-1, keepdims=True)
    softmax_low = (exponent / totals).astype(jnp.bfloat16)
    mixture = jnp.einsum(
        "hqk,khd->qhd", softmax_low, value_heads, preferred_element_type=jnp.float32
    )
    log_totals = (highest + jnp.log(totals))[..., 0]
    return (mixture.reshape(row_count, HEADS * HD).astype(jnp.bfloat16), log_totals)


def attend_backward(operands):
    queries, keys_all, values_all, allowed, log_totals, grad_mixture = operands
    row_count = queries.shape[0]
    key_count = keys_all.shape[0]
    query_heads = queries.reshape(row_count, HEADS, HD)
    key_heads = keys_all.reshape(key_count, HEADS, HD)
    value_heads = values_all.reshape(key_count, HEADS, HD)
    grad_heads = grad_mixture.reshape(row_count, HEADS, HD)
    masked = score_block(query_heads, key_heads, allowed)
    softmax_out = jnp.exp(masked - log_totals[..., None])
    softmax_low = softmax_out.astype(jnp.bfloat16)
    grad_vals = jnp.einsum(
        "hqk,qhd->khd", softmax_low, grad_heads, preferred_element_type=jnp.float32
    )
    grad_soft = jnp.einsum(
        "qhd,khd->hqk", grad_heads, value_heads, preferred_element_type=jnp.float32
    )
    inner_sum = jnp.sum(softmax_out * grad_soft, axis=-1, keepdims=True)
    grad_scores = (softmax_out * (grad_soft - inner_sum)).astype(jnp.bfloat16)
    grad_query = jnp.einsum(
        "hqk,khd->qhd", grad_scores, key_heads, preferred_element_type=jnp.float32
    ) * HD ** (-0.5)
    grad_key = jnp.einsum(
        "hqk,qhd->khd", grad_scores, query_heads, preferred_element_type=jnp.float32
    ) * HD ** (-0.5)
    return (
        grad_query.reshape(row_count, HEADS * HD).astype(jnp.bfloat16),
        grad_key.reshape(key_count, HEADS * HD),
        grad_vals.reshape(key_count, HEADS * HD),
    )


def column_sum(values):
    return jnp.sum(values.astype(jnp.float32), axis=0)


def on_device(
    activations,
    cotangent,
    segment_ids,
    inputs_weight,
    inputs_moment,
    inputs_second,
    output_weight,
    output_moment,
    output_second,
    expand_weight,
    expand_moment,
    expand_second,
    reduce_weight,
    reduce_moment,
    reduce_second,
    vector_params,
    vector_moment,
    vector_second,
):
    gathered = (
        lax.all_gather(inputs_weight.astype(jnp.bfloat16), "seq", axis=0, tiled=True),
        lax.all_gather(output_weight.astype(jnp.bfloat16), "seq", axis=0, tiled=True),
        lax.all_gather(expand_weight.astype(jnp.bfloat16), "seq", axis=0, tiled=True),
        lax.all_gather(reduce_weight.astype(jnp.bfloat16), "seq", axis=0, tiled=True),
        lax.all_gather(vector_params.astype(jnp.bfloat16), "seq", axis=1, tiled=True),
    )
    inputs_low, output_low, expand_low, reduce_low, vector_low = gathered
    vectors = vector_low.astype(jnp.float32)
    features = vectors.shape[1]
    seqs_here = activations.shape[0]
    local_len = activations.shape[1]
    key_count = segment_ids.shape[1]
    rows_here = seqs_here * local_len
    own_index = lax.axis_index("seq")
    residual_in = activations.astype(jnp.float32).reshape(rows_here, features)
    normed_value, norm_back_one = jax.vjp(layer_norm, residual_in, vectors[0], vectors[1])
    normed_one = normed_value.astype(jnp.bfloat16)
    projected = jnp.dot(normed_one, inputs_low, preferred_element_type=jnp.float32)
    queries = (projected[:, :features] + vectors[4]).astype(jnp.bfloat16)
    keys_here = projected[:, features : 2 * features].astype(jnp.bfloat16)
    values_here = (projected[:, 2 * features :] + vectors[5]).astype(jnp.bfloat16)
    key_blocks = keys_here.reshape(seqs_here, local_len, features)
    value_blocks = values_here.reshape(seqs_here, local_len, features)
    keys_all, values_all = (
        lax.all_gather(key_blocks, "seq", axis=1, tiled=True),
        lax.all_gather(value_blocks, "seq", axis=1, tiled=True),
    )
    offset = own_index * local_len
    segments_here = lax.dynamic_slice_in_dim(segment_ids, offset, local_len, 1)
    query_places = offset + jnp.arange(local_len, dtype=jnp.int32)
    key_places = jnp.arange(key_count, dtype=jnp.int32)
    causal = query_places[:, None] >= key_places[None, :]
    allowed = causal[None] & (segments_here[:, :, None] == segment_ids[:, None, :])
    query_blocks = queries.reshape(seqs_here, local_len, features)
    mixture, log_totals = lax.map(attend_forward, (query_blocks, keys_all, values_all, allowed))
    mixture_rows = mixture.reshape(rows_here, features)
    attended = jnp.dot(mixture_rows, output_low, preferred_element_type=jnp.float32) + vectors[6]
    middle = residual_in + attended
    normed_value_two, norm_back_two = jax.vjp(layer_norm, middle, vectors[2], vectors[3])
    normed_two = normed_value_two.astype(jnp.bfloat16)
    expanded = jnp.dot(normed_two, expand_low, preferred_element_type=jnp.float32) + vectors[
        8:
    ].reshape(-1)
    gelu_value, gelu_back = jax.vjp(partial(jax.nn.gelu, approximate=False), expanded)
    hidden_low = gelu_value.astype(jnp.bfloat16)
    reduced = jnp.dot(hidden_low, reduce_low, preferred_element_type=jnp.float32) + vectors[7]
    layer_output = (middle + reduced).astype(jnp.bfloat16).reshape(activations.shape)
    grad_top = cotangent.reshape(rows_here, features)
    grad_reduce = contract_rows(hidden_low, grad_top)
    grad_hidden = contract_cols(grad_top, reduce_low)
    grad_expanded = gelu_back(grad_hidden)[0].astype(jnp.bfloat16)
    grad_expand = contract_rows(normed_two, grad_expanded)
    grad_normed_two = contract_cols(grad_expanded, expand_low)
    grad_middle_norm, grad_gain_two, grad_shift_two = norm_back_two(grad_normed_two)
    grad_middle = grad_top.astype(jnp.float32) + grad_middle_norm
    grad_attended = grad_middle.astype(jnp.bfloat16)
    grad_output = contract_rows(mixture_rows, grad_attended)
    grad_mixture = contract_cols(grad_attended, output_low).astype(jnp.bfloat16)
    grad_queries, grad_keys_all, grad_values_all = lax.map(
        attend_backward,
        (
            query_blocks,
            keys_all,
            values_all,
            allowed,
            log_totals,
            grad_mixture.reshape(seqs_here, local_len, features),
        ),
    )
    grad_keys, grad_values = (
        lax.psum_scatter(
            grad_keys_all.astype(jnp.bfloat16), "seq", scatter_dimension=1, tiled=True
        ).astype(jnp.float32),
        lax.psum_scatter(
            grad_values_all.astype(jnp.bfloat16), "seq", scatter_dimension=1, tiled=True
        ).astype(jnp.float32),
    )
    grad_query_rows = grad_queries.reshape(rows_here, features)
    grad_value_rows = grad_values.reshape(rows_here, features).astype(jnp.bfloat16)
    grad_projected = jnp.concatenate(
        [
            grad_query_rows,
            grad_keys.reshape(rows_here, features).astype(jnp.bfloat16),
            grad_value_rows,
        ],
        axis=1,
    )
    grad_inputs = contract_rows(normed_one, grad_projected)
    grad_normed_one = contract_cols(grad_projected, inputs_low)
    grad_residual, grad_gain_one, grad_shift_one = norm_back_one(grad_normed_one)
    input_grad = (grad_middle + grad_residual).astype(jnp.bfloat16).reshape(activations.shape)
    head_rows = jnp.stack(
        [
            grad_gain_one,
            grad_shift_one,
            grad_gain_two,
            grad_shift_two,
            column_sum(grad_query_rows),
            column_sum(grad_value_rows),
            column_sum(grad_attended),
            column_sum(grad_top),
        ]
    )
    grad_vectors = jnp.concatenate(
        [head_rows, column_sum(grad_expanded).reshape(-1, features)], axis=0
    )
    group_sums = (
        lax.psum_scatter(
            grad_inputs.astype(jnp.bfloat16), "seq", scatter_dimension=0, tiled=True
        ).astype(jnp.float32),
        lax.psum_scatter(
            grad_output.astype(jnp.bfloat16), "seq", scatter_dimension=0, tiled=True
        ).astype(jnp.float32),
        lax.psum_scatter(
            grad_expand.astype(jnp.bfloat16), "seq", scatter_dimension=0, tiled=True
        ).astype(jnp.float32),
        lax.psum_scatter(
            grad_reduce.astype(jnp.bfloat16), "seq", scatter_dimension=0, tiled=True
        ).astype(jnp.float32),
        lax.psum_scatter(
            grad_vectors.astype(jnp.bfloat16), "seq", scatter_dimension=1, tiled=True
        ).astype(jnp.float32),
    )
    grad_inputs, grad_output, grad_expand, grad_reduce, grad_vectors = lax.psum(
        (group_sums[0], group_sums[1], group_sums[2], group_sums[3], group_sums[4]), "dp"
    )
    new_inputs = adamw_step(
        inputs_weight, inputs_moment, inputs_second, grad_inputs, 0.03, decay_rate
    )
    new_output = adamw_step(
        output_weight, output_moment, output_second, grad_output, 0.3, decay_rate
    )
    new_expand = adamw_step(
        expand_weight, expand_moment, expand_second, grad_expand, 0.03, decay_rate
    )
    new_reduce = adamw_step(
        reduce_weight, reduce_moment, reduce_second, grad_reduce, 0.02, decay_rate
    )
    new_vectors = adamw_step(vector_params, vector_moment, vector_second, grad_vectors, 0.5, 0.0)
    return (
        layer_output,
        input_grad,
        new_inputs[0],
        new_inputs[1],
        new_inputs[2],
        new_output[0],
        new_output[1],
        new_output[2],
        new_expand[0],
        new_expand[1],
        new_expand[2],
        new_reduce[0],
        new_reduce[1],
        new_reduce[2],
        new_vectors[0],
        new_vectors[1],
        new_vectors[2],
    )


def solution(mesh):
    in_specs = (
        P("dp", "seq", None),
        P("dp", "seq", None),
        P("dp", None),
        P("seq", None),
        P("seq", None),
        P("seq", None),
        P("seq", None),
        P("seq", None),
        P("seq", None),
        P("seq", None),
        P("seq", None),
        P("seq", None),
        P("seq", None),
        P("seq", None),
        P("seq", None),
        P(None, "seq"),
        P(None, "seq"),
        P(None, "seq"),
    )
    out_specs = (
        P("dp", "seq", None),
        P("dp", "seq", None),
        P("seq", None),
        P("seq", None),
        P("seq", None),
        P("seq", None),
        P("seq", None),
        P("seq", None),
        P("seq", None),
        P("seq", None),
        P("seq", None),
        P("seq", None),
        P("seq", None),
        P("seq", None),
        P(None, "seq"),
        P(None, "seq"),
        P(None, "seq"),
    )
    return jax.shard_map(
        on_device, mesh=mesh, in_specs=in_specs, out_specs=out_specs, check_vma=False
    )
```

profile of v0, /device:TPU:9, one launch (start us, length us, event | category | flops | bytes accessed | tf_op | source)
XLA Modules:
  0.0 1133.4 jit_solution(5356313415419759122)
XLA Ops:
  11.1 10.5 all-gather
  22.6 56.4 %all-gather.8.cloned.1.call-done = bf16[768,2304]{1,0:T(8,128)(2,1)} async-done(((bf16[192,2304]{1,0:T(8,128)(2,1)}), bf16[768,2304]{1,0:T(8,128)(2,1)}) %all-gather.8.cloned.1.call-update) | async-done | bytes 3538960 | tf_op jit(solution)/shard_map/all_gather | solution.py:132
  101.6 46.6 %all-gather.12.cloned.1.call-done = bf16[2,1024,768]{1,2,0:T(8,128)(2,1)} async-done(((bf16[2,256,768]{1,2,0:T(8,128)(2,1)}), bf16[2,1024,768]{1,2,0:T(8,128)(2,1)}) %all-gather.12.cloned.1.call-update) | async-done | bytes 3145744 | tf_op jit(solution)/shard_map/all_gather | solution.py:156
  148.2 63.8 %all-gather.10.cloned.1.call-done = bf16[2,1024,768]{1,2,0:T(8,128)(2,1)} async-done(((bf16[2,256,768]{1,2,0:T(8,128)(2,1)}), bf16[2,1024,768]{1,2,0:T(8,128)(2,1)}) %all-gather.10.cloned.1.call-update) | async-done | bytes 3145744 | tf_op jit(solution)/shard_map/all_gather | solution.py:157
  212.0 28.7 %while.26 = (s32[]{:T(128)}, bf16[2,256,768]{2,1,0:T(8,128)(2,1)S(1)}, f32[2,12,256]{2,1,0:T(8,128)S(1)}, bf16[2,1024,768]{1,2,0:T(8,128)(2,1)}, pred[2,256,1024...) while((s32[]{:T(128)}, ...), condition=%wide.region_5.6_spmd, body=%wide.region_2.5_spmd.sunk | while | flops 843248640 | bytes 51753072 | solution.py:166
  240.7 4.0 all-gather.14.cloned.1.call-done
  247.5 86.0 %all-gather.16.cloned.1.call-done = bf16[768,3072]{1,0:T(8,128)(2,1)} async-done(((bf16[192,3072]{1,0:T(8,128)(2,1)}), bf16[768,3072]{1,0:T(8,128)(2,1)}) %all-gather.16.cloned.1.call-update) | async-done | bytes 4718608 | tf_op jit(solution)/shard_map/all_gather | solution.py:134
  333.5 7.1 fusion.44
  340.6 82.8 %all-gather.18.cloned.1.call-done = bf16[3072,768]{1,0:T(8,128)(2,1)} async-done(((bf16[768,768]{1,0:T(8,128)(2,1)}), bf16[3072,768]{1,0:T(8,128)(2,1)}) %all-gather.18.cloned.1.call-update) | async-done | bytes 4718608 | tf_op jit(solution)/shard_map/all_gather | solution.py:135
  423.4 21.0 %fusion.51 = (bf16[3072]{0:T(1024)(128)(2,1)}, bf16[512,3072]{1,0:T(8,128)(2,1)S(1)}, f32[512,3072]{1,0:T(8,128)}) fusion(f32[512,3072]{1,0:T(8,128)} %fusion.44, f32[3072]{0:T(1024)S(1)} %add.260, bf16[512,768]{1,0:T(8,128)(2,1)S(1)} %bitcast.183, bf16[3072,768]{1,0:T(8,128)(2,1)} %all-gather.18.cloned.1.call-done), kind=kOutput, calls=%fused_computation.137 | convolution fusion | flops 2532307968 | bytes 21252096 | tf_op jit(solution)/shard_map/dot_general | solution.py:35
  452.1 89.6 %while.27 = (s32[]{:T(128)}, bf16[2,256,768]{1,2,0:T(8,128)(2,1)}, bf16[2,1024,768]{2,1,0:T(8,128)(2,1)}, bf16[2,1024,768]{2,1,0:T(8,128)(2,1)}, bf16[2,1024,768...) while((s32[]{:T(128)}, bf16[2,256,768]{1,2,0:T(8,128)(2,1)}, ...), condition=%wide.region_12.13_spmd, body=%wide.region_10.12_spmd.sunk | while | flops 2062414848 | bytes 246305200 | solution.py:190
  460.5 5.2 fusion.128
  467.5 12.1 %multiply_reduce_fusion.5 = (f32[12,256]{1,0:T(8,128)S(1)}, f32[12,256,1024]{2,1,0:T(8,128)}) fusion(f32[12,256,1024]{2,1,0:T(8,128)} %copy-done, f32[12,256]{1,0:T(8,128)S(1)} %dynamic-slice_bitcast_fusion.7, pred[256,1024]{1,0:T(8,128)(4,1)} %copy-done.3, bf16[256,12,64]{0,2,1:T(8,128)(2,1)} %bitcast.181, bf16[1024,12,64]{0,2,1:T(8,128)(2,1)} %bitcast.173), kind=kOutput, calls=%fused_computation.16.clone.1 | convolution fusion | flops 418378752 | bytes 27418624 | tf_op jit(solution)/shard_map/while/body/eval_jaxpr/qhd,khd->hqk/dot_general | solution.py:89
  480.7 6.7 multiply_convert_fusion.3
  505.2 5.2 fusion.128
  512.2 12.1 %multiply_reduce_fusion.5 = (f32[12,256]{1,0:T(8,128)S(1)}, f32[12,256,1024]{2,1,0:T(8,128)}) fusion(f32[12,256,1024]{2,1,0:T(8,128)} %copy-done, f32[12,256]{1,0:T(8,128)S(1)} %dynamic-slice_bitcast_fusion.7, pred[256,1024]{1,0:T(8,128)(4,1)} %copy-done.3, bf16[256,12,64]{0,2,1:T(8,128)(2,1)} %bitcast.181, bf16[1024,12,64]{0,2,1:T(8,128)(2,1)} %bitcast.173), kind=kOutput, calls=%fused_computation.16.clone.1 | convolution fusion | flops 418378752 | bytes 27418624 | tf_op jit(solution)/shard_map/while/body/eval_jaxpr/qhd,khd->hqk/dot_general | solution.py:89
  525.4 6.7 multiply_convert_fusion.3
  546.1 56.7 %reduce-scatter.12.cloned.1.call-done = bf16[2,256,768]{2,1,0:T(8,128)(2,1)} async-done(((bf16[2,1024,768]{2,1,0:T(8,128)(2,1)}), bf16[2,256,768]{2,1,0:T(8,128)(2,1)}) %reduce-scatter.12.cloned.1.call-update) | async-done | bytes 786448 | tf_op jit(solution)/shard_map/reduce_scatter | solution.py:205
  604.1 61.3 %reduce-scatter.10.cloned.1.call-done = bf16[2,256,768]{2,1,0:T(8,128)(2,1)} async-done(((bf16[2,1024,768]{2,1,0:T(8,128)(2,1)}), bf16[2,256,768]{2,1,0:T(8,128)(2,1)}) %reduce-scatter.10.cloned.1.call-update) | async-done | bytes 786448 | tf_op jit(solution)/shard_map/reduce_scatter | solution.py:202
  665.4 4.6 fusion.45
  673.1 6.5 convolution_convert_fusion.1
  680.3 6.2 multiply_convert_fusion.1
  688.1 4.4 convolution_convert_fusion
  693.9 5.3 convolution_convert_fusion.2
  699.8 7.3 add_convert_fusion.2
  715.6 89.1 %reduce-scatter.18.cloned.1.call-done = bf16[192,3072]{1,0:T(8,128)(2,1)} async-done(((bf16[768,3072]{1,0:T(8,128)(2,1)}), bf16[192,3072]{1,0:T(8,128)(2,1)}) %reduce-scatter.18.cloned.1.call-update) | async-done | bytes 1179664 | tf_op jit(solution)/shard_map/reduce_scatter | solution.py:245
  804.7 88.1 %reduce-scatter.20.cloned.1.call-done = bf16[768,768]{1,0:T(8,128)(2,1)} async-done(((bf16[3072,768]{1,0:T(8,128)(2,1)}), bf16[768,768]{1,0:T(8,128)(2,1)}) %reduce-scatter.20.cloned.1.call-update) | async-done | bytes 1179664 | tf_op jit(solution)/shard_map/reduce_scatter | solution.py:248
  892.8 69.1 %reduce-scatter.14.cloned.1.call-done = bf16[192,2304]{1,0:T(8,128)(2,1)} async-done(((bf16[768,2304]{1,0:T(8,128)(2,1)}), bf16[192,2304]{1,0:T(8,128)(2,1)}) %reduce-scatter.14.cloned.1.call-update) | async-done | bytes 884752 | tf_op jit(solution)/shard_map/reduce_scatter | solution.py:239
  961.9 143.7 %all-reduce.2 = (f32[192,2304]{1,0:T(8,128)}, f32[192,768]{1,0:T(8,128)}, f32[192,3072]{1,0:T(8,128)}, f32[768,768]{1,0:T(8,128)S(1)}, f32[12,192]{1,0:T(8,128)}) all-reduce(bf16[192,2304]{1,0:T(8,128)(2,1)} %reduce-scatter.14.cloned.1.call-done, ...), channel_id=1, replica_groups=mesh['dp'=8,'seq'=4] {'dp'}, use_global_device_ids=true, to_apply=%region_18.19 | all-reduce | flops 1771776 | bytes 10630656 | tf_op jit(solution)/shard_map/psum | solution.py:255
  1109.9 5.5 multiply_subtract_fusion.2
  1116.7 4.6 multiply_subtract_fusion.1
  1122.3 4.1 multiply_subtract_fusion
  (304 shorter events, 135.0 us)
Async XLA Ops:
  7.2 71.9 %all-gather.8.cloned.1.call-start = ((), (), s32[]{:S(2)}) async-start(), calls=%async_computation.7 | async-start | bytes 4423680 | tf_op jit(solution)/shard_map/all_gather | solution.py:132
  9.8 138.4 %all-gather.12.cloned.1.call-start = ((), (), s32[]{:S(2)}) async-start(), calls=%async_computation.9 | async-start | bytes 3932160 | tf_op jit(solution)/shard_map/all_gather | solution.py:156
  10.1 73.0 %copy-start.46 = (f32[1,2,2,128]{3,1,2,0:T(2,128)}, f32[1,2,2,128]{3,1,2,0:T(2,128)S(1)}, u32[]{:S(2)}) copy-start(f32[1,2,2,128]{3,1,2,0:T(2,128)S(1)} %copy.86) | copy-start | bytes 6148
  11.1 72.0 %copy-start.48 = (f32[512]{0:T(512)}, f32[512]{0:T(512)S(1)}, u32[]{:S(2)}) copy-start(f32[512]{0:T(512)S(1)} %rsqrt.20) | copy-start | bytes 6148
  22.3 60.8 %copy-start.42 = (f32[768]{0:T(1024)}, f32[768]{0:T(1024)S(1)}, u32[]{:S(2)}) copy-start(f32[768]{0:T(1024)S(1)} %get-tuple-element.179) | copy-start | bytes 9220
  22.3 311.2 %copy-start.64 = (f32[768]{0:T(1024)}, f32[768]{0:T(1024)S(1)}, u32[]{:S(2)}) copy-start(f32[768]{0:T(1024)S(1)} %get-tuple-element.173) | copy-start | bytes 9220
  22.3 425.6 %copy-start.56 = (f32[768]{0:T(1024)}, f32[768]{0:T(1024)S(1)}, u32[]{:S(2)}) copy-start(f32[768]{0:T(1024)S(1)} %get-tuple-element.174) | copy-start | bytes 9220
  22.6 56.4 %copy-start.31 = (bf16[512,768]{1,0:T(8,128)(2,1)}, bf16[512,768]{1,0:T(8,128)(2,1)S(1)}, u32[]{:S(2)}) copy-start(bf16[512,768]{1,0:T(8,128)(2,1)S(1)} %fusion.30) | copy-start | bytes 2359300
  86.5 125.5 %all-gather.10.cloned.1.call-start = ((), (), s32[]{:S(2)}) async-start(), calls=%async_computation.8 | async-start | bytes 3932160 | tf_op jit(solution)/shard_map/all_gather | solution.py:157
  92.3 152.5 %all-gather.14.cloned.1.call-start = ((), (), s32[]{:S(2)}) async-start(), calls=%async_computation.10 | async-start | bytes 1474560 | tf_op jit(solution)/shard_map/all_gather | solution.py:133
  94.2 239.3 %all-gather.16.cloned.1.call-start = ((), (), s32[]{:S(2)}) async-start(), calls=%async_computation.11 | async-start | bytes 5898240 | tf_op jit(solution)/shard_map/all_gather | solution.py:134
  95.5 327.9 %all-gather.18.cloned.1.call-start = ((), (), s32[]{:S(2)}) async-start(), calls=%async_computation.12 | async-start | bytes 5898240 | tf_op jit(solution)/shard_map/all_gather | solution.py:135
  98.5 504.2 %reduce-scatter.12.cloned.1.call-start = ((), (), s32[]{:S(2)}) async-start(), calls=%async_computation.14 | async-start | bytes 3932160 | tf_op jit(solution)/shard_map/reduce_scatter | solution.py:205
  99.0 324.4 %copy-start.44 = (f32[3072]{0:T(1024)}, f32[3072]{0:T(1024)S(1)}, u32[]{:S(2)}) copy-start(f32[3072]{0:T(1024)S(1)} %add.260) | copy-start | bytes 36868
  247.1 200.8 %copy-start.17 = (f32[512,768]{1,0:T(8,128)}, f32[512,768]{1,0:T(8,128)S(1)}, u32[]{:S(2)}) copy-start(f32[512,768]{1,0:T(8,128)S(1)} %get-tuple-element.254) | copy-start | bytes 4718596
  247.2 200.8 %copy-start.52 = (f32[512]{0:T(512)}, f32[512]{0:T(512)S(1)}, u32[]{:S(2)}) copy-start(f32[512]{0:T(512)S(1)} %broadcast_multiply_fusion) | copy-start | bytes 6148
  247.5 200.5 %copy-start.59 = (f32[512]{0:T(512)}, f32[512]{0:T(512)S(1)}, u32[]{:S(2)}) copy-start(f32[512]{0:T(512)S(1)} %fusion.39) | copy-start | bytes 6148
  333.5 89.9 %copy-start.15 = (bf16[2,256,768]{2,1,0:T(8,128)(2,1)S(1)}, bf16[2,256,768]{2,1,0:T(8,128)(2,1)}, u32[]{:S(2)}) copy-start(bf16[2,256,768]{2,1,0:T(8,128)(2,1)} %param.23) | copy-start | bytes 2359300
  423.4 21.0 %copy-start.68 = (bf16[768,3072]{1,0:T(8,128)(2,1)S(1)}, bf16[768,3072]{1,0:T(8,128)(2,1)}, u32[]{:S(2)}) copy-start(bf16[768,3072]{1,0:T(8,128)(2,1)} %all-gather.16.cloned.1.call-done) | copy-start | bytes 14155780
  541.8 123.6 %reduce-scatter.10.cloned.1.call-start = ((), (), s32[]{:S(2)}) async-start(), calls=%async_computation.13 | async-start | bytes 3932160 | tf_op jit(solution)/shard_map/reduce_scatter | solution.py:202
  542.6 164.6 %reduce-scatter.16.cloned.1.call-start = ((), (), s32[]{:S(2)}) async-start(), calls=%async_computation.16 | async-start | bytes 1474560 | tf_op jit(solution)/shard_map/reduce_scatter | solution.py:242
  545.0 120.4 %copy-start.8 = (bf16[2,256,768]{2,1,0:T(8,128)(2,1)S(1)}, bf16[2,256,768]{2,1,0:T(8,128)(2,1)}, u32[]{:S(2)}) copy-start(bf16[2,256,768]{2,1,0:T(8,128)(2,1)} %param.22) | copy-start | bytes 2359300
  545.0 120.4 %copy-start.43 = (f32[768]{0:T(1024)S(1)}, f32[768]{0:T(1024)}, u32[]{:S(2)}) copy-start(f32[768]{0:T(1024)} %copy-done.42) | copy-start | bytes 9220
  545.0 120.4 %copy-start.47 = (f32[1,2,2,128]{3,1,2,0:T(2,128)S(1)}, f32[1,2,2,128]{3,1,2,0:T(2,128)}, u32[]{:S(2)}) copy-start(f32[1,2,2,128]{3,1,2,0:T(2,128)} %copy-done.46) | copy-start | bytes 6148
  545.0 169.1 %reduce-scatter.22.cloned.1.call-start = ((), (), s32[]{:S(2)}) async-start(), calls=%async_computation.19 | async-start | bytes 245760
  545.9 119.5 %copy-start.33 = (bf16[2,256,768]{2,1,0:T(8,128)(2,1)}, bf16[2,256,768]{2,1,0:T(8,128)(2,1)S(1)}, u32[]{:S(2)}) copy-start(bf16[2,256,768]{2,1,0:T(8,128)(2,1)S(1)} %copy.57) | copy-start | bytes 2359300
  673.0 131.7 %reduce-scatter.18.cloned.1.call-start = ((), (), s32[]{:S(2)}) async-start(), calls=%async_computation.17 | async-start | bytes 5898240 | tf_op jit(solution)/shard_map/reduce_scatter | solution.py:245
  679.6 213.2 %reduce-scatter.20.cloned.1.call-start = ((), (), s32[]{:S(2)}) async-start(), calls=%async_computation.18 | async-start | bytes 5898240 | tf_op jit(solution)/shard_map/reduce_scatter | solution.py:248
  692.5 269.4 %reduce-scatter.14.cloned.1.call-start = ((), (), s32[]{:S(2)}) async-start(), calls=%async_computation.15 | async-start | bytes 4423680 | tf_op jit(solution)/shard_map/reduce_scatter | solution.py:239
  710.2 395.4 %copy-start.41 = (f32[12,192]{1,0:T(8,128)S(1)}, f32[12,192]{1,0:T(8,128)}, u32[]{:S(2)}) copy-start(f32[12,192]{1,0:T(8,128)} %param.37) | copy-start | bytes 27652
  710.2 396.9 %copy-start.24 = (f32[192,768]{1,0:T(8,128)S(1)}, f32[192,768]{1,0:T(8,128)}, u32[]{:S(2)}) copy-start(f32[192,768]{1,0:T(8,128)} %param.28) | copy-start | bytes 1769476
  710.2 396.9 %copy-start.37 = (f32[192,768]{1,0:T(8,128)S(1)}, f32[192,768]{1,0:T(8,128)}, u32[]{:S(2)}) copy-start(f32[192,768]{1,0:T(8,128)} %param.29) | copy-start | bytes 1769476
  (63 other events, 266.4 us)
Sparse Core Ops, SparseCore 0:
  10.2 68.8 all-gather.7
  86.6 61.5 all-gather.11
  150.3 61.5 all-gather.9
  214.0 30.7 all-gather.13
  246.7 86.6 all-gather.15
  335.5 87.8 all-gather.17
  541.9 60.8 reduce-scatter.11
  605.1 60.2 reduce-scatter.9
  668.3 27.6 reduce-scatter.15
  698.6 15.4 reduce-scatter.21
  716.5 88.1 reduce-scatter.17
  807.0 85.7 reduce-scatter.19
  895.2 66.6 reduce-scatter.13
where the time goes:
time: 1140 us; the launch traced here: 1130 us
  waiting for transfers between devices  709 us (62%)
  blocking collectives  154 us (14%)
  matrix products  128 us (11%)
  other arithmetic  66.9 us (6%)
  local copies, waits for them, and re-layouts  58.5 us (5%)
  between operations  15.1 us (1%)
    psum x1, blocking collectives, on_device(): lax.psum((group_sums[0], group_sums[1], group_sums[2], group_sums[3], gro...  144 us
    reduce_scatter x1, waiting for transfers between devices, on_device(): lax.psum_scatter(grad_expand.astype(jnp.bfloat16), 'seq', scatter_dimensi...  89.1 us
    reduce_scatter x1, waiting for transfers between devices, on_device(): lax.psum_scatter(grad_reduce.astype(jnp.bfloat16), 'seq', scatter_dimensi...  88.1 us
    all_gather x1, waiting for transfers between devices, on_device(): lax.all_gather(expand_weight.astype(jnp.bfloat16), 'seq', axis=0, tiled=T...  86 us
    all_gather x1, waiting for transfers between devices, on_device(): lax.all_gather(reduce_weight.astype(jnp.bfloat16), 'seq', axis=0, tiled=T...  82.8 us
    reduce_scatter x1, waiting for transfers between devices, on_device(): lax.psum_scatter(grad_inputs.astype(jnp.bfloat16), 'seq', scatter_dimensi...  69.1 us
    all_gather x1, waiting for transfers between devices, on_device(): lax.all_gather(value_blocks, 'seq', axis=1, tiled=True)  63.8 us
    reduce_scatter x1, waiting for transfers between devices, on_device(): lax.psum_scatter(grad_keys_all.astype(jnp.bfloat16), 'seq', scatter_dimen...  61.3 us
  transfers between devices with their start and end apart: 13, of which 12 were waited for; matrix products, arithmetic and copies ran while one was open for 9% of the time, Pallas kernels for 0%

commit v1 on v0

v1 whole, which is shorter than its diff:
```python
from functools import partial

import jax
import jax.numpy as jnp
from jax import lax
from jax.experimental import pallas as pl
from jax.experimental.pallas import tpu as pltpu
from jax.sharding import PartitionSpec as P

HEADS = 12
HD = 64
STEP = 10
PAIR = 2 * HD
LANES = 128

eps_norm = 1e-05
eps_adam = 1e-08
beta_one = 0.9
beta_two = 0.95
decay_rate = 0.1
mask_fill = -1e30
vmem_bytes = 56 * 1024 * 1024

VISIBLE = (
    (0, 256, 0, 256),
    (256, 256, 128, 512),
    (512, 256, 128, 768),
    (768, 128, 128, 896),
    (896, 128, 768, 1024),
)
TILE_STARTS = []
tile_total = 0
for _first, _rows, _low, _high in VISIBLE:
    TILE_STARTS.append(tile_total)
    tile_total += _high - _low

low = jnp.bfloat16


def dot_nn(left_side, right_side):
    return lax.dot_general(
        left_side, right_side, (((1,), (0,)), ((), ())), preferred_element_type=jnp.float32
    )


def dot_tn(left_side, right_side):
    return lax.dot_general(
        left_side, right_side, (((0,), (0,)), ((), ())), preferred_element_type=jnp.float32
    )


def dot_nt(left_side, right_side):
    return lax.dot_general(
        left_side, right_side, (((1,), (1,)), ((), ())), preferred_element_type=jnp.float32
    )


def normalize(values):
    center = jnp.mean(values, axis=-1, keepdims=True)
    offsets = values - center
    spread = jnp.mean(offsets * offsets, axis=-1, keepdims=True)
    inverse = lax.rsqrt(spread + eps_norm)
    return offsets * inverse, inverse


def norm_back(grad_normed, gain, unit, inverse):
    scaled = grad_normed * gain
    mean_scaled = jnp.mean(scaled, axis=-1, keepdims=True)
    mean_cross = jnp.mean(scaled * unit, axis=-1, keepdims=True)
    return inverse * (scaled - mean_scaled - unit * mean_cross)


def adamw_step(weight, moment, second, gradient, step_rate, weight_decay):
    moment_new = beta_one * moment + (1.0 - beta_one) * gradient
    second_new = beta_two * second + (1.0 - beta_two) * gradient * gradient
    fix_one = 1.0 - beta_one**STEP
    fix_two = 1.0 - beta_two**STEP
    update = moment_new / fix_one / (jnp.sqrt(second_new / fix_two) + eps_adam)
    return (weight - step_rate * (update + weight_decay * weight), moment_new, second_new)


def column_sum(values):
    return jnp.sum(values.astype(jnp.float32), axis=0)


def fill_bias(seg_row, seg_col, bias):
    for (first, rows, key_low, key_high), start in zip(VISIBLE, TILE_STARTS):
        keys = key_high - key_low
        key_places = key_low + lax.broadcasted_iota(jnp.int32, (keys, rows), 0)
        query_places = first + lax.broadcasted_iota(jnp.int32, (keys, rows), 1)
        same = seg_col[key_low:key_high, :] == seg_row[:, first : first + rows]
        allowed = same & (key_places <= query_places)
        bias[start : start + keys, 0:rows] = jnp.where(allowed, 0.0, mask_fill)


def lane_masks(shape):
    lane = lax.broadcasted_iota(jnp.int32, shape, 1)
    return (lane < HD, lane >= HD)


def masked_to(values, mask):
    return jnp.where(mask, values, jnp.zeros_like(values))


def attend_forward_kernel(seg_row, seg_col, q_ref, k_ref, v_ref, out_ref, log_ref, bias):
    @pl.when(pl.program_id(0) == 0)
    def _():
        fill_bias(seg_row, seg_col, bias)

    masks = lane_masks((k_ref.shape[0], PAIR))
    keys_masked = [masked_to(k_ref[...], mask) for mask in masks]
    for (first, rows, key_low, key_high), start in zip(VISIBLE, TILE_STARTS):
        queries = q_ref[first : first + rows, :] * jnp.asarray(HD**-0.5, low)
        values = v_ref[key_low:key_high, :]
        mixed = []
        for head in range(2):
            scores = dot_nt(keys_masked[head][key_low:key_high], queries)
            scores = scores + bias[start : start + key_high - key_low, 0:rows]
            highest = jnp.max(scores, axis=0, keepdims=True)
            exponent = jnp.exp(scores - highest)
            totals = jnp.sum(exponent, axis=0, keepdims=True)
            soft = (exponent * (1.0 / totals)).astype(low)
            mixed.append(dot_tn(soft, values))
            log_ref[0, head : head + 1, first : first + rows] = highest + jnp.log(totals)
        half = lane_masks((rows, PAIR))[0]
        out_ref[first : first + rows, :] = jnp.where(half, mixed[0], mixed[1]).astype(low)


def attend_backward_kernel(
    seg_row, seg_col, q_ref, k_ref, v_ref, log_ref, do_ref, dq_ref, dk_ref, dv_ref, bias, dk_acc, dv_acc
):
    @pl.when(pl.program_id(0) == 0)
    def _():
        fill_bias(seg_row, seg_col, bias)

    masks = lane_masks((k_ref.shape[0], PAIR))
    keys_masked = [masked_to(k_ref[...], mask) for mask in masks]
    values_masked = [masked_to(v_ref[...], mask) for mask in masks]
    dk_acc[...] = jnp.zeros_like(dk_acc)
    dv_acc[...] = jnp.zeros_like(dv_acc)
    for (first, rows, key_low, key_high), start in zip(VISIBLE, TILE_STARTS):
        queries = q_ref[first : first + rows, :] * jnp.asarray(HD**-0.5, low)
        grads = do_ref[first : first + rows, :]
        grad_query = jnp.zeros((rows, PAIR), jnp.float32)
        row_masks = lane_masks((rows, PAIR))
        for head in range(2):
            keys = keys_masked[head][key_low:key_high]
            scores = dot_nt(keys, queries)
            scores = scores + bias[start : start + key_high - key_low, 0:rows]
            soft = jnp.exp(scores - log_ref[0, head : head + 1, first : first + rows])
            grad_soft = dot_nt(values_masked[head][key_low:key_high], grads)
            inner = jnp.sum(soft * grad_soft, axis=0, keepdims=True)
            grad_scores = (soft * (grad_soft - inner)).astype(low)
            dv_acc[key_low:key_high, :] += dot_nn(
                soft.astype(low), masked_to(grads, row_masks[head])
            )
            dk_acc[key_low:key_high, :] += dot_nn(
                grad_scores, masked_to(queries, row_masks[head])
            )
            grad_query = grad_query + dot_tn(grad_scores, keys)
        dq_ref[first : first + rows, :] = (grad_query * HD**-0.5).astype(low)
    dk_ref[...] = dk_acc[...].astype(low)
    dv_ref[...] = dv_acc[...].astype(low)


def attend_specs(length, pairs):
    whole = lambda shape: pl.BlockSpec(shape, lambda j: (0,) * len(shape))
    columns = lambda offset: pl.BlockSpec((length, PAIR), lambda j, offset=offset: (0, offset + j))
    logs = pl.BlockSpec((1, 8, length), lambda j: (j, 0, 0))
    return whole, columns, logs


def attend_forward(seg_row, seg_col, projected):
    length = projected.shape[0]
    pairs = projected.shape[1] // (3 * PAIR)
    whole, columns, logs = attend_specs(length, pairs)
    return pl.pallas_call(
        attend_forward_kernel,
        grid=(pairs,),
        in_specs=[
            whole((1, length)),
            whole((length, 1)),
            columns(0),
            columns(pairs),
            columns(2 * pairs),
        ],
        out_specs=[columns(0), logs],
        out_shape=[
            jax.ShapeDtypeStruct((length, pairs * PAIR), low),
            jax.ShapeDtypeStruct((pairs, 8, length), jnp.float32),
        ],
        scratch_shapes=[pltpu.VMEM((tile_total, 256), jnp.float32)],
        compiler_params=pltpu.CompilerParams(vmem_limit_bytes=vmem_bytes),
        cost_estimate=pl.CostEstimate(
            flops=4 * length * length * pairs * PAIR, bytes_accessed=8 * length * pairs * PAIR,
            transcendentals=length * length * pairs,
        ),
        name="attend_forward",
    )(seg_row, seg_col, projected, projected, projected)


def attend_backward(seg_row, seg_col, projected, logs_all, grad_mixture):
    length = projected.shape[0]
    pairs = projected.shape[1] // (3 * PAIR)
    whole, columns, logs = attend_specs(length, pairs)
    return pl.pallas_call(
        attend_backward_kernel,
        grid=(pairs,),
        in_specs=[
            whole((1, length)),
            whole((length, 1)),
            columns(0),
            columns(pairs),
            columns(2 * pairs),
            logs,
            columns(0),
        ],
        out_specs=[columns(0)] * 3,
        out_shape=[jax.ShapeDtypeStruct((length, pairs * PAIR), low)] * 3,
        scratch_shapes=[
            pltpu.VMEM((tile_total, 256), jnp.float32),
            pltpu.VMEM((length, PAIR), jnp.float32),
            pltpu.VMEM((length, PAIR), jnp.float32),
        ],
        compiler_params=pltpu.CompilerParams(vmem_limit_bytes=vmem_bytes),
        cost_estimate=pl.CostEstimate(
            flops=10 * length * length * pairs * PAIR, bytes_accessed=14 * length * pairs * PAIR,
            transcendentals=length * length * pairs,
        ),
        name="attend_backward",
    )(seg_row, seg_col, projected, projected, projected, logs_all, grad_mixture)


def feed_kernel(
    n2_ref, dy_ref, wu_ref, wd_ref, bu_ref, red_ref, dn2_ref, gu_ref, gd_ref, dbu_ref, n2_turned
):
    step = pl.program_id(0)

    @pl.when(step == 0)
    def _():
        n2_turned[...] = n2_ref[...].T
        red_ref[...] = jnp.zeros_like(red_ref)
        dn2_ref[...] = jnp.zeros_like(dn2_ref)

    normed = n2_ref[...]
    grad_top = dy_ref[...]
    expanded = dot_nn(normed, wu_ref[...]) + bu_ref[...]
    phi = 0.5 + 0.5 * lax.erf(expanded * (0.5**0.5))
    density = jnp.exp(-0.5 * expanded * expanded) * 0.3989422804014327
    hidden = (expanded * phi).astype(low)
    slope = phi + expanded * density
    grad_hidden = dot_nt(grad_top, wd_ref[...])
    grad_expanded = grad_hidden * slope
    grad_low = grad_expanded.astype(low)
    red_ref[...] += dot_nn(hidden, wd_ref[...])
    dn2_ref[...] += dot_nt(grad_low, wu_ref[...])
    gu_ref[...] = dot_nn(n2_turned[...], grad_low).astype(low)
    gd_ref[...] = dot_tn(hidden, grad_top).astype(low)
    dbu_ref[...] = jnp.sum(grad_low.astype(jnp.float32), axis=0, keepdims=True)


def feed_both(normed, grad_top, expand_low, reduce_low, expand_bias):
    rows, features = normed.shape
    hidden_count = reduce_low.shape[0]
    block = 512
    whole = pl.BlockSpec((rows, features), lambda j: (0, 0))
    across = pl.BlockSpec((features, block), lambda j: (0, j))
    down = pl.BlockSpec((block, features), lambda j: (j, 0))
    bias = pl.BlockSpec((1, block), lambda j: (0, j))
    return pl.pallas_call(
        feed_kernel,
        grid=(hidden_count // block,),
        in_specs=[whole, whole, across, down, bias],
        out_specs=[whole, whole, across, down, bias],
        out_shape=[
            jax.ShapeDtypeStruct((rows, features), jnp.float32),
            jax.ShapeDtypeStruct((rows, features), jnp.float32),
            jax.ShapeDtypeStruct((features, hidden_count), low),
            jax.ShapeDtypeStruct((hidden_count, features), low),
            jax.ShapeDtypeStruct((1, hidden_count), jnp.float32),
        ],
        scratch_shapes=[pltpu.VMEM((features, rows), low)],
        compiler_params=pltpu.CompilerParams(vmem_limit_bytes=vmem_bytes),
        cost_estimate=pl.CostEstimate(
            flops=12 * rows * features * hidden_count,
            bytes_accessed=8 * features * hidden_count,
            transcendentals=2 * rows * hidden_count,
        ),
        name="feed_both",
    )(normed, grad_top, expand_low, reduce_low, expand_bias)


def chip_routes(dp_count, seq_count):
    straight, crossed = [], []
    for place in range(dp_count):
        group, core = place - place % 2, place % 2
        for quarter in range(seq_count):
            source = place * seq_count + quarter
            holder = (group + quarter // 2) * seq_count
            straight.append((source, holder + 2 * core + quarter % 2))
            crossed.append((source, holder + 2 * core + 1 - quarter % 2))
    return straight, crossed


def on_device(
    dp_count,
    seq_count,
    activations,
    cotangent,
    segment_ids,
    inputs_weight,
    inputs_moment,
    inputs_second,
    output_weight,
    output_moment,
    output_second,
    expand_weight,
    expand_moment,
    expand_second,
    reduce_weight,
    reduce_moment,
    reduce_second,
    vector_params,
    vector_moment,
    vector_second,
):
    axes = ("dp", "seq")
    everyone = ("seq", "dp")
    dp_index = lax.axis_index("dp")
    seq_index = lax.axis_index("seq")
    core = dp_index % 2
    odd = seq_index % 2
    features = activations.shape[2]
    quarter = activations.shape[1]
    vector_rows = vector_params.shape[0]
    straight, crossed = chip_routes(dp_count, seq_count)
    core_pairs = [(place, place ^ 1) for place in range(dp_count)]

    def to_chip(values):
        near = lax.dynamic_index_in_dim(values, odd, 0, keepdims=False)
        far = lax.dynamic_index_in_dim(values, 1 - odd, 0, keepdims=False)
        near = lax.ppermute(near, axes, straight)
        far = lax.ppermute(far, axes, crossed)
        return jnp.concatenate(
            [jnp.where(odd == 0, near, far), jnp.where(odd == 0, far, near)], axis=0
        )

    def from_chip(values):
        near = lax.dynamic_slice_in_dim(values, odd * quarter, quarter, 0)
        far = lax.dynamic_slice_in_dim(values, (1 - odd) * quarter, quarter, 0)
        near = lax.ppermute(near, axes, [(there, here) for here, there in straight])
        far = lax.ppermute(far, axes, [(there, here) for here, there in crossed])
        return jnp.stack([jnp.where(odd == 0, near, far), jnp.where(odd == 0, far, near)])

    def swap_cores(values):
        return lax.ppermute(values, "dp", core_pairs)

    def own_piece(weight):
        rows = weight.shape[0] // dp_count
        return lax.dynamic_slice_in_dim(weight, dp_index * rows, rows, 0).astype(low)

    def spread(piece):
        return lax.all_gather(piece, everyone, axis=0, tiled=True)

    vector_piece = jnp.pad(own_piece(vector_params.T), ((0, 0), (0, LANES - vector_rows)))
    first_low = spread(
        jnp.concatenate([own_piece(inputs_weight), own_piece(output_weight), vector_piece], axis=1)
    )
    expand_low = spread(own_piece(expand_weight))
    reduce_low = spread(own_piece(reduce_weight))
    wide = 3 * features
    inputs_low = first_low[:, :wide]
    output_low = first_low[:, wide : wide + features]
    vectors = first_low[:, wide + features : wide + features + vector_rows].T.astype(jnp.float32)

    residual_low = to_chip(activations)
    grad_top = to_chip(cotangent)
    rows_here = residual_low.shape[0]
    other_segments = swap_cores(segment_ids)
    segment_pair = jnp.where(seq_index // 2 == core, segment_ids, other_segments)
    segments = lax.dynamic_index_in_dim(segment_pair, odd, 0, keepdims=False)
    seg_row, seg_col = segments[None, :], segments[:, None]

    residual = residual_low.astype(jnp.float32)
    unit_one, inverse_one = normalize(residual)
    normed_one = (unit_one * vectors[0] + vectors[1]).astype(low)
    projected = dot_nn(normed_one, inputs_low)
    queries = (projected[:, :features] + vectors[4]).astype(low)
    keys = projected[:, features : 2 * features].astype(low)
    values = (projected[:, 2 * features :] + vectors[5]).astype(low)
    half = features // 2
    group_low = jnp.concatenate([queries[:, :half], keys[:, :half], values[:, :half]], axis=1)
    group_high = jnp.concatenate([queries[:, half:], keys[:, half:], values[:, half:]], axis=1)

    def join_tokens(mine, theirs):
        return jnp.where(
            core == 0,
            jnp.concatenate([mine, theirs], axis=0),
            jnp.concatenate([theirs, mine], axis=0),
        )

    def tokens_of(values, which):
        return lax.dynamic_slice_in_dim(values, which * rows_here, rows_here, 0)

    mine = jnp.where(core == 0, group_low, group_high)
    theirs = swap_cores(jnp.where(core == 0, group_high, group_low))
    projected_heads = join_tokens(mine, theirs)
    mixture_heads, logs_all = attend_forward(seg_row, seg_col, projected_heads)
    mixture_mine = tokens_of(mixture_heads, core)
    mixture_theirs = swap_cores(tokens_of(mixture_heads, 1 - core))
    mixture = jnp.where(
        core == 0,
        jnp.concatenate([mixture_mine, mixture_theirs], axis=1),
        jnp.concatenate([mixture_theirs, mixture_mine], axis=1),
    )

    middle = residual + (dot_nn(mixture, output_low) + vectors[6])
    unit_two, inverse_two = normalize(middle)
    normed_two = (unit_two * vectors[2] + vectors[3]).astype(low)
    reduced, grad_normed_two, grad_expand, grad_reduce, bias_sums = feed_both(
        normed_two, grad_top, expand_low, reduce_low, vectors[8:].reshape(1, -1)
    )
    layer_output = from_chip((middle + (reduced + vectors[7])).astype(low))
    expand_part = lax.psum_scatter(grad_expand, everyone, scatter_dimension=0, tiled=True)
    reduce_part = lax.psum_scatter(grad_reduce, everyone, scatter_dimension=0, tiled=True)

    grad_middle = grad_top.astype(jnp.float32) + norm_back(
        grad_normed_two, vectors[2], unit_two, inverse_two
    )
    grad_attended = grad_middle.astype(low)
    grad_output = dot_tn(mixture, grad_attended).astype(low)
    grad_mixture = dot_nt(grad_attended, output_low).astype(low)
    grad_mine = jnp.where(core == 0, grad_mixture[:, :half], grad_mixture[:, half:])
    grad_theirs = swap_cores(jnp.where(core == 0, grad_mixture[:, half:], grad_mixture[:, :half]))
    grad_heads = attend_backward(
        seg_row, seg_col, projected_heads, logs_all, join_tokens(grad_mine, grad_theirs)
    )
    grad_all = jnp.concatenate(grad_heads, axis=1)
    back_mine = tokens_of(grad_all, core)
    back_theirs = swap_cores(tokens_of(grad_all, 1 - core))
    back_low = jnp.where(core == 0, back_mine, back_theirs)
    back_high = jnp.where(core == 0, back_theirs, back_mine)
    grad_projected = jnp.concatenate(
        [
            part[:, start : start + half]
            for start in (0, half, 2 * half)
            for part in (back_low, back_high)
        ],
        axis=1,
    )
    grad_inputs = dot_tn(normed_one, grad_projected).astype(low)
    grad_normed_one = dot_nt(grad_projected, inputs_low)
    grad_residual = norm_back(grad_normed_one, vectors[0], unit_one, inverse_one)
    input_grad = from_chip((grad_middle + grad_residual).astype(low))

    head_rows = jnp.stack(
        [
            column_sum(grad_normed_one * unit_one),
            column_sum(grad_normed_one),
            column_sum(grad_normed_two * unit_two),
            column_sum(grad_normed_two),
            column_sum(grad_projected[:, :features]),
            column_sum(grad_projected[:, 2 * features :]),
            column_sum(grad_attended),
            column_sum(grad_top),
        ]
    )
    grad_vectors = jnp.concatenate([head_rows, bias_sums.reshape(-1, features)], axis=0)
    vector_columns = jnp.pad(grad_vectors.T.astype(low), ((0, 0), (0, LANES - vector_rows)))
    first_part = lax.psum_scatter(
        jnp.concatenate([grad_inputs, grad_output, vector_columns], axis=1),
        everyone,
        scatter_dimension=0,
        tiled=True,
    )

    def regather(part):
        return lax.all_gather(part, "dp", axis=0, tiled=True).astype(jnp.float32)

    sum_expand = regather(expand_part)
    sum_reduce = regather(reduce_part)
    sum_first = regather(first_part)
    sum_inputs = sum_first[:, :wide]
    sum_output = sum_first[:, wide : wide + features]
    sum_vectors = sum_first[:, wide + features : wide + features + vector_rows].T

    new_inputs = adamw_step(
        inputs_weight, inputs_moment, inputs_second, sum_inputs, 0.03, decay_rate
    )
    new_output = adamw_step(
        output_weight, output_moment, output_second, sum_output, 0.3, decay_rate
    )
    new_expand = adamw_step(
        expand_weight, expand_moment, expand_second, sum_expand, 0.03, decay_rate
    )
    new_reduce = adamw_step(
        reduce_weight, reduce_moment, reduce_second, sum_reduce, 0.02, decay_rate
    )
    new_vectors = adamw_step(vector_params, vector_moment, vector_second, sum_vectors, 0.5, 0.0)
    return (
        layer_output,
        input_grad,
        *new_inputs,
        *new_output,
        *new_expand,
        *new_reduce,
        *new_vectors,
    )


def solution(mesh):
    tokens = P("dp", "seq", None)
    rows = P("seq", None)
    columns = P(None, "seq")
    in_specs = (tokens, tokens, P("dp", None)) + (rows,) * 12 + (columns,) * 3
    out_specs = (tokens, tokens) + (rows,) * 12 + (columns,) * 3
    return jax.shard_map(
        partial(on_device, mesh.shape["dp"], mesh.shape["seq"]),
        mesh=mesh,
        in_specs=in_specs,
        out_specs=out_specs,
        check_vma=False,
    )
```

time: 1140 us -> 686 us (0.60)
  waiting for transfers between devices: 709 us -> 464 us
  blocking collectives: 154 us -> 0 us
  matrix products: 128 us -> 18.6 us
  Pallas kernels: 0 us -> 43.9 us
  starting transfers between devices: 1.04 us -> 22.3 us
  other arithmetic: 66.9 us -> 53.7 us
    reduce_scatter x6 -> x2, waiting for transfers between devices: 364 us -> 161 us  [the longest x1 112 us: on_device(): lax.psum_scatter(grad_expand, everyone, scatter_dimension=0, tiled=True)]
    all_gather x6, waiting for transfers between devices: 340 us -> 192 us  [the longest x3 128 us: spread(): return lax.all_gather(piece, everyone, axis=0, tiled=True)]
    psum x1 -> x0, blocking collectives: 144 us -> none  [on_device(): lax.psum((group_sums[0], group_sums[1], group_sums[2], group_sums[3], gro...]
    dot_general x26 -> x6, matrix products: 128 us -> 18.6 us  [the longest x2 6.43 us: dot_nn(): lax.dot_general(left_side, right_side, (((1,), (0,)), ((), ())), preferre...]
    unnamed x14 -> x10, waiting for transfers between devices: 4.78 us -> 60.4 us
    ppermute x0 -> x13, waiting for transfers between devices: none -> 50.8 us  [the longest x2 16.2 us: to_chip(): near = lax.ppermute(near, axes, straight)]
    pallas_call x0 -> x3, Pallas kernels: none -> 43.9 us  [the longest x1 19.6 us: feed_both(): pl.pallas_call(feed_kernel, grid=(hidden_count // block,), in_specs=[whol...]
    convert_element_type x10 -> x5, other arithmetic: 34.8 us -> 4.84 us  [the longest x1 1.83 us: regather(): return lax.all_gather(part, 'dp', axis=0, tiled=True).astype(jnp.float32)]
  transfers between devices with their start and end apart: 13 -> 22, of which waited for: 12 -> 15; matrix products, arithmetic and copies ran while one was open for 9% -> 14% of each run, Pallas kernels for 0% -> 4%
where the time goes in v1:
time: 686 us; the launch traced here: 679 us
  waiting for transfers between devices  464 us (68%)
  local copies, waits for them, and re-layouts  60.9 us (9%)
  other arithmetic  53.7 us (8%)
  Pallas kernels  43.9 us (6%)
  starting transfers between devices  22.3 us (3%)
  matrix products  18.6 us (3%)
  between operations  15 us (2%)
    all_gather x3, waiting for transfers between devices, spread(): return lax.all_gather(piece, everyone, axis=0, tiled=True)  128 us
    reduce_scatter x1, waiting for transfers between devices, on_device(): lax.psum_scatter(grad_expand, everyone, scatter_dimension=0, tiled=True)  112 us
    all_gather x3, waiting for transfers between devices, regather(): return lax.all_gather(part, 'dp', axis=0, tiled=True).astype(jnp.float32)  64 us
    unnamed x10, waiting for transfers between devices  60.4 us
    reduce_scatter x1, waiting for transfers between devices, on_device(): lax.psum_scatter(grad_reduce, everyone, scatter_dimension=0, tiled=True)  48.8 us
    unnamed x111, local copies, waits for them, and re-layouts  36.5 us
    sub x5, other arithmetic, adamw_step(): weight - step_rate * (update + weight_decay * weight)  24.2 us
    pallas_call x1, Pallas kernels, feed_both(): pl.pallas_call(feed_kernel, grid=(hidden_count // block,), in_specs=[whol...  19.6 us
  transfers between devices with their start and end apart: 22, of which 15 were waited for; matrix products, arithmetic and copies ran while one was open for 14% of the time, Pallas kernels for 4%

profile of v1, /device:TPU:9, one launch (start us, length us, event | category | flops | bytes accessed | tf_op | source)
XLA Modules:
  0.0 678.7 jit_solution(352101811998990602)
XLA Ops:
  14.4 4.8 collective-permute-start
  19.2 16.2 %collective-permute-done = bf16[256,768]{1,0:T(8,128)(2,1)S(1)} collective-permute-done((bf16[256,768]{1,0:T(8,128)(2,1)S(1)}, bf16[256,768]{1,0:T(8,128)(2,1)S(1)}, u32[]{:S(2)}, u32[]{:S(2)}) %collective-permute-start) | collective-permute-done | bytes 393248 | tf_op jit(solution)/shard_map/ppermute | solution.py:342
  35.5 4.3 collective-permute-done.1
  40.4 42.9 %all-gather.7.cloned.1.call-done = bf16[768,3200]{1,0:T(8,128)(2,1)} async-done(((bf16[24,3200]{1,0:T(8,128)(2,1)}), bf16[768,3200]{1,0:T(8,128)(2,1)}) %all-gather.7.cloned.1.call-update) | async-done | bytes 4915216 | tf_op jit(solution)/shard_map/all_gather | solution.py:363
  86.4 4.2 fusion.55
  101.6 9.2 %attend_forward.1 = (bf16[1024,384]{1,0:T(8,128)(2,1)}, f32[3,8,1024]{2,1,0:T(8,128)}) custom-call(s32[1,1024]{1,0:T(1,128)} %copy-done.24, s32[1024,1]{1,0:T(8,128)} %copy.111.seg_col, bf16[1024,1152]{1,0:T(8,128)(2,1)} %maximum_select_fusion.q_ref.k_ref.v_ref, bf16[1024,1152]{1,0:T(8,128)(2,1)} %maximum_select_fusion.q_ref.k_ref.v_ref, ...), custom_call_target="tpu_custom_call" | custom-call | flops 1610612736 | bytes 3145728 | tf_op jit(solution)/shard_map/attend_forward/pallas_call | solution.py:177
  113.7 10.1 %collective-permute-done.6 = bf16[256,768]{1,0:T(8,128)(2,1)} collective-permute-done((bf16[256,768]{1,0:T(8,128)(2,1)}, bf16[256,768]{1,0:T(8,128)(2,1)}, u32[]{:S(2)}, u32[]{:S(2)}) %collective-permute-start.6) | collective-permute-done | bytes 393248 | tf_op jit(solution)/shard_map/ppermute | solution.py:343
  131.5 19.2 %all-gather.9.cloned.1.call-done.wu_ref = bf16[768,3072]{1,0:T(8,128)(2,1)} async-done(((bf16[24,3072]{1,0:T(8,128)(2,1)}), bf16[768,3072]{1,0:T(8,128)(2,1)}) %all-gather.9.cloned.1.call-update) | async-done | bytes 4718608 | tf_op jit(solution)/shard_map/all_gather | solution.py:363
  150.7 66.0 %all-gather.11.cloned.1.call-done.wd_ref = bf16[3072,768]{1,0:T(8,128)(2,1)} async-done(((bf16[96,768]{1,0:T(8,128)(2,1)}), bf16[3072,768]{1,0:T(8,128)(2,1)}) %all-gather.11.cloned.1.call-update) | async-done | bytes 4718608 | tf_op jit(solution)/shard_map/all_gather | solution.py:363
  216.7 19.6 %feed_both.1 = (f32[512,768]{1,0:T(8,128)}, f32[512,768]{1,0:T(8,128)}, bf16[768,3072]{1,0:T(8,128)(2,1)}, bf16[3072,768]{1,0:T(8,128)(2,1)}, f32[1,3072]{1,0:T(1,128)}) custom-call(bf16[512,768]{1,0:T(8,128)(2,1)} %add_convert_fusion.1.n2_ref, bf16[512,768]{1,0:T(8,128)(2,1)} %pad_maximum_fusion.3.dy_ref, ...), custom_call_target="tpu_custom_call" | custom-call | flops 14495514624 | bytes 18874368 | tf_op jit(solution)/shard_map/feed_both/pallas_call | solution.py:270
  237.7 3.8 multiply_reduce_fusion
  247.9 15.2 %attend_backward.1 = (bf16[1024,384]{1,0:T(8,128)(2,1)}, bf16[1024,384]{1,0:T(8,128)(2,1)}, bf16[1024,384]{1,0:T(8,128)(2,1)}) custom-call(s32[1,1024]{1,0:T(1,128)} %copy-done.24, s32[1024,1]{1,0:T(8,128)} %copy.111.seg_col, bf16[1024,1152]{1,0:T(8,128)(2,1)} %maximum_select_fusion.q_ref.k_ref.v_ref, ...), custom_call_target="tpu_custom_call" | custom-call | flops 4026531840 | bytes 5505024 | tf_op jit(solution)/shard_map/attend_backward/pallas_call | solution.py:206
  276.4 4.0 fusion.24
  285.1 4.0 convolution_convert_fusion
  291.8 48.8 %reduce-scatter.8.cloned.1.call-done = bf16[96,768]{1,0:T(8,128)(2,1)} async-done(((bf16[3072,768]{1,0:T(8,128)(2,1)}), bf16[96,768]{1,0:T(8,128)(2,1)}) %reduce-scatter.8.cloned.1.call-update) | async-done | bytes 147472 | tf_op jit(solution)/shard_map/reduce_scatter | solution.py:425
  340.7 112.2 %reduce-scatter.6.cloned.1.call-done = bf16[24,3072]{1,0:T(8,128)(2,1)} async-done(((bf16[768,3072]{1,0:T(8,128)(2,1)}), bf16[24,3072]{1,0:T(8,128)(2,1)}) %reduce-scatter.6.cloned.1.call-update) | async-done | bytes 147472 | tf_op jit(solution)/shard_map/reduce_scatter | solution.py:424
  453.2 3.0 copy.120
  457.4 3.0 copy.114
  460.4 2.9 copy.118
  467.9 5.7 collective-permute-start.7
  475.8 4.5 collective-permute-start.11
  480.4 3.0 collective-permute-done.7
  483.4 16.0 %collective-permute-done.8 = bf16[256,768]{1,0:T(8,128)(2,1)S(1)} collective-permute-done((bf16[256,768]{1,0:T(8,128)(2,1)S(1)}, bf16[256,768]{1,0:T(8,128)(2,1)S(1)}, u32[]{:S(2)}, u32[]{:S(2)}) %collective-permute-start.8) | collective-permute-done | bytes 393248 | tf_op jit(solution)/shard_map/ppermute | solution.py:352
  500.4 60.2 %reduce-scatter.10.cloned.1.call-done = bf16[24,3200]{1,0:T(8,128)(2,1)} async-done(((bf16[768,3200]{1,0:T(8,128)(2,1)}), bf16[24,3200]{1,0:T(8,128)(2,1)}) %reduce-scatter.10.cloned.1.call-update) | async-done | bytes 153616
  562.7 26.1 %all-gather.17.cloned.1.call-done = bf16[768,768]{1,0:T(8,128)(2,1)} async-done(((bf16[96,768]{1,0:T(8,128)(2,1)}), bf16[768,768]{1,0:T(8,128)(2,1)}) %all-gather.17.cloned.1.call-update) | async-done | bytes 1179664 | tf_op jit(solution)/shard_map/all_gather | solution.py:478
  588.7 6.8 %multiply_subtract_fusion = (f32[768,768]{1,0:T(8,128)}, f32[768,768]{1,0:T(8,128)}, f32[768,768]{1,0:T(8,128)}) fusion(f32[768,768]{1,0:T(8,128)S(1)} %copy-done.13, bf16[768,768]{1,0:T(8,128)(2,1)} %all-gather.17.cloned.1.call-done, f32[768,768]{1,0:T(8,128)} %param.31, f32[768,768]{1,0:T(8,128)} %param.32), kind=kLoop, calls=%fused_computation.22 | loop fusion | flops 9437184 | bytes 15335424 | tf_op jit(solution)/shard_map/sub | solution.py:79
  595.6 19.3 %all-gather.15.cloned.1.call-done = bf16[192,3072]{1,0:T(8,128)(2,1)} async-done(((bf16[24,3072]{1,0:T(8,128)(2,1)}), bf16[192,3072]{1,0:T(8,128)(2,1)}) %all-gather.15.cloned.1.call-update) | async-done | bytes 1179664 | tf_op jit(solution)/shard_map/all_gather | solution.py:478
  614.9 7.7 %multiply_subtract_fusion.1 = (f32[192,3072]{1,0:T(8,128)}, f32[192,3072]{1,0:T(8,128)}, f32[192,3072]{1,0:T(8,128)}) fusion(f32[192,3072]{1,0:T(8,128)} %param.27, bf16[192,3072]{1,0:T(8,128)(2,1)} %all-gather.15.cloned.1.call-done, f32[192,3072]{1,0:T(8,128)} %param.28, f32[192,3072]{1,0:T(8,128)} %param.29), kind=kLoop, calls=%fused_computation.23 | loop fusion | flops 9437184 | bytes 15335424 | tf_op jit(solution)/shard_map/sub | solution.py:79
  622.5 18.7 %all-gather.13.cloned.1.call-done = bf16[192,3200]{1,0:T(8,128)(2,1)} async-done(((bf16[24,3200]{1,0:T(8,128)(2,1)}), bf16[192,3200]{1,0:T(8,128)(2,1)}) %all-gather.13.cloned.1.call-update) | async-done | bytes 1228816 | tf_op jit(solution)/shard_map/all_gather | solution.py:478
  646.7 5.7 multiply_subtract_fusion.2
  652.4 2.9 copy.125
  661.1 3.4 multiply_subtract_fusion.3
  (217 shorter events, 90.6 us)
Async XLA Ops:
  7.2 7.1 %copy-start.17 = (bf16[2,256,768]{2,1,0:T(8,128)(2,1)S(1)}, bf16[2,256,768]{2,1,0:T(8,128)(2,1)}, u32[]{:S(2)}) copy-start(bf16[2,256,768]{2,1,0:T(8,128)(2,1)} %param.18) | copy-start | bytes 2359300
  7.2 76.1 %all-gather.7.cloned.1.call-start = ((), (), s32[]{:S(2)}) async-start(), calls=%async_computation.3 | async-start | bytes 5068800 | tf_op jit(solution)/shard_map/all_gather | solution.py:363
  10.8 139.9 %all-gather.9.cloned.1.call-start = ((), (), s32[]{:S(2)}) async-start(), calls=%async_computation.4 | async-start | bytes 4866048 | tf_op jit(solution)/shard_map/all_gather | solution.py:363
  12.5 204.2 %all-gather.11.cloned.1.call-start = ((), (), s32[]{:S(2)}) async-start(), calls=%async_computation.5 | async-start | bytes 4866048 | tf_op jit(solution)/shard_map/all_gather | solution.py:363
  14.2 326.4 %reduce-scatter.8.cloned.1.call-start = ((), (), s32[]{:S(2)}) async-start(), calls=%async_computation.9 | async-start | bytes 4866048 | tf_op jit(solution)/shard_map/reduce_scatter | solution.py:425
  14.4 21.1 %collective-permute-start = (bf16[256,768]{1,0:T(8,128)(2,1)S(1)}, bf16[256,768]{1,0:T(8,128)(2,1)S(1)}, u32[]{:S(2)}, u32[]{:S(2)}) collective-permute-start(bf16[256,768]{1,0:T(8,128)(2,1)S(1)} %get-tuple-element.196), channel_id=1, source_target_pairs={{0,0},{1,1},{2,4},{3,5},{4,2},{5,3},{6,6},{7,7},{8,8},{9,9},{10,12... | collective-permute-start | bytes 1179656 | tf_op jit(solution)/shard_map/ppermute | solution.py:342
  19.1 20.6 %collective-permute-start.1 = (bf16[256,768]{1,0:T(8,128)(2,1)S(1)}, bf16[256,768]{1,0:T(8,128)(2,1)S(1)}, u32[]{:S(2)}, u32[]{:S(2)}) collective-permute-start(bf16[256,768]{1,0:T(8,128)(2,1)S(1)} %get-tuple-element.197), channel_id=1, source_target_pairs={{0,1},{1,0},{2,5},{3,4},{4,3},{5,2},{6,7},{7,6},{8,9},{9,8},{10,13... | collective-permute-start | bytes 1179656 | tf_op jit(solution)/shard_map/ppermute | solution.py:343
  39.8 87.8 %copy-start.4 = (bf16[256,768]{1,0:T(8,128)(2,1)}, bf16[256,768]{1,0:T(8,128)(2,1)S(1)}, u32[]{:S(2)}) copy-start(bf16[256,768]{1,0:T(8,128)(2,1)S(1)} %get-tuple-element.195) | copy-start | bytes 1179652
  40.4 46.0 %copy-start.34 = (f32[512]{0:T(512)}, f32[512]{0:T(512)S(1)}, u32[]{:S(2)}) copy-start(f32[512]{0:T(512)S(1)} %add_rsqrt_fusion.1) | copy-start | bytes 6148
  92.5 6.7 collective-permute-start.3
  92.8 4.7 collective-permute-start.2
  94.0 19.7 %collective-permute-start.5 = (bf16[256,768]{1,0:T(8,128)(2,1)}, bf16[256,768]{1,0:T(8,128)(2,1)}, u32[]{:S(2)}, u32[]{:S(2)}) collective-permute-start(bf16[256,768]{1,0:T(8,128)(2,1)} %get-tuple-element.186), channel_id=1, source_target_pairs={{0,0},{1,1},{2,4},{3,5},{4,2},{5,3},{6,6},{7,7},{8,8},{9,9},{10,12... | collective-permute-start | bytes 1179656 | tf_op jit(solution)/shard_map/ppermute | solution.py:342
  96.7 27.1 %collective-permute-start.6 = (bf16[256,768]{1,0:T(8,128)(2,1)}, bf16[256,768]{1,0:T(8,128)(2,1)}, u32[]{:S(2)}, u32[]{:S(2)}) collective-permute-start(bf16[256,768]{1,0:T(8,128)(2,1)} %get-tuple-element.187), channel_id=1, source_target_pairs={{0,1},{1,0},{2,5},{3,4},{4,3},{5,2},{6,7},{7,6},{8,9},{9,8},{10,13... | collective-permute-start | bytes 1179656 | tf_op jit(solution)/shard_map/ppermute | solution.py:343
  112.0 15.7 %copy-start.21 = (bf16[512,384]{1,0:T(8,128)(2,1)}, bf16[512,384]{1,0:T(8,128)(2,1)S(1)}, u32[]{:S(2)}) copy-start(bf16[512,384]{1,0:T(8,128)(2,1)S(1)} %get-tuple-element.188) | copy-start | bytes 1179652
  112.0 15.7 %collective-permute-start.4 = (bf16[512,384]{1,0:T(8,128)(2,1)S(1)}, bf16[512,384]{1,0:T(8,128)(2,1)S(1)}, u32[]{:S(2)}, u32[]{:S(2)}) collective-permute-start(bf16[512,384]{1,0:T(8,128)(2,1)S(1)} %get-tuple-element.189), channel_id=1, source_target_pairs={{0,4},{4,0},{8,12},{12,8},{16,20},{20,16},{24,28},{28,24},{1,5},{5... | collective-permute-start | bytes 1179656 | tf_op jit(solution)/shard_map/ppermute | solution.py:356
  236.3 216.6 %reduce-scatter.6.cloned.1.call-start = ((), (), s32[]{:S(2)}) async-start(), calls=%async_computation.7 | async-start | bytes 4866048 | tf_op jit(solution)/shard_map/reduce_scatter | solution.py:424
  244.9 1.8 collective-permute-start.9
  245.2 315.4 %reduce-scatter.10.cloned.1.call-start = ((), (), s32[]{:S(2)}) async-start(), calls=%async_computation.11 | async-start | bytes 5068800
  267.4 4.8 collective-permute-start.10
  291.8 297.0 %all-gather.17.cloned.1.call-start = ((), (), s32[]{:S(2)}) async-start(), calls=%async_computation.10 | async-start | bytes 1327104 | tf_op jit(solution)/shard_map/all_gather | solution.py:478
  340.6 274.2 %all-gather.15.cloned.1.call-start = ((), (), s32[]{:S(2)}) async-start(), calls=%async_computation.8 | async-start | bytes 1327104 | tf_op jit(solution)/shard_map/all_gather | solution.py:478
  452.9 188.3 %all-gather.13.cloned.1.call-start = ((), (), s32[]{:S(2)}) async-start(), calls=%async_computation.6 | async-start | bytes 1382400 | tf_op jit(solution)/shard_map/all_gather | solution.py:478
  465.6 9.5 %copy-start.36 = (f32[512]{0:T(512)S(1)}, f32[512]{0:T(512)}, u32[]{:S(2)}) copy-start(f32[512]{0:T(512)} %copy-done.34) | copy-start | bytes 6148
  467.9 7.2 %copy-start.14 = (f32[512,768]{1,0:T(8,128)S(1)}, f32[512,768]{1,0:T(8,128)}, u32[]{:S(2)}) copy-start(f32[512,768]{1,0:T(8,128)} %get-tuple-element.202) | copy-start | bytes 4718596
  467.9 15.4 %collective-permute-start.7 = (bf16[256,768]{1,0:T(8,128)(2,1)S(1)}, bf16[256,768]{1,0:T(8,128)(2,1)S(1)}, u32[]{:S(2)}, u32[]{:S(2)}) collective-permute-start(bf16[256,768]{1,0:T(8,128)(2,1)S(1)} %get-tuple-element.182), channel_id=1, source_target_pairs={{0,0},{1,1},{4,2},{5,3},{2,4},{3,5},{6,6},{7,7},{8,8},{9,9},{12,10... | collective-permute-start | bytes 1179656 | tf_op jit(solution)/shard_map/ppermute | solution.py:351
  473.6 25.7 %collective-permute-start.8 = (bf16[256,768]{1,0:T(8,128)(2,1)S(1)}, bf16[256,768]{1,0:T(8,128)(2,1)S(1)}, u32[]{:S(2)}, u32[]{:S(2)}) collective-permute-start(bf16[256,768]{1,0:T(8,128)(2,1)S(1)} %get-tuple-element.183), channel_id=1, source_target_pairs={{1,0},{0,1},{5,2},{4,3},{3,4},{2,5},{7,6},{6,7},{9,8},{8,9},{13,10... | collective-permute-start | bytes 1179656 | tf_op jit(solution)/shard_map/ppermute | solution.py:352
  475.8 84.9 %collective-permute-start.11 = (bf16[256,768]{1,0:T(8,128)(2,1)S(1)}, bf16[256,768]{1,0:T(8,128)(2,1)S(1)}, u32[]{:S(2)}, u32[]{:S(2)}) collective-permute-start(bf16[256,768]{1,0:T(8,128)(2,1)S(1)} %get-tuple-element.176), channel_id=1, source_target_pairs={{0,0},{1,1},{4,2},{5,3},{2,4},{3,5},{6,6},{7,7},{8,8},{9,9},{12,10... | collective-permute-start | bytes 1179656 | tf_op jit(solution)/shard_map/ppermute | solution.py:351
  480.3 80.4 %collective-permute-start.12 = (bf16[256,768]{1,0:T(8,128)(2,1)S(1)}, bf16[256,768]{1,0:T(8,128)(2,1)}, u32[]{:S(2)}, u32[]{:S(2)}) collective-permute-start(bf16[256,768]{1,0:T(8,128)(2,1)S(1)} %get-tuple-element.177), channel_id=1, source_target_pairs={{1,0},{0,1},{5,2},{4,3},{3,4},{2,5},{7,6},{6,7},{9,8},{8,9},{13,10... | collective-permute-start | bytes 1179656 | tf_op jit(solution)/shard_map/ppermute | solution.py:352
  500.4 88.3 %copy-start.13 = (f32[768,768]{1,0:T(8,128)S(1)}, f32[768,768]{1,0:T(8,128)}, u32[]{:S(2)}) copy-start(f32[768,768]{1,0:T(8,128)} %param.30) | copy-start | bytes 7077892
  664.5 6.6 copy-start.25
  664.5 6.6 copy-start.27
  664.5 6.6 copy-start.28
  (36 other events, 108.7 us)
Sparse Core Ops, SparseCore 0:
  11.5 71.7 all-gather.6
  86.8 63.8 all-gather.8
  154.2 62.4 all-gather.10
  236.4 104.1 reduce-scatter.7
  346.8 106.0 reduce-scatter.5
  458.5 102.1 reduce-scatter.9
  562.7 26.0 all-gather.16
  590.8 24.0 all-gather.14
  616.9 24.2 all-gather.12

commit v2 on v1

--- a/solution.py
+++ b/solution.py
@@ -231,63 +231,90 @@
     )(seg_row, seg_col, projected, projected, projected, logs_all, grad_mixture)
 
 
-def feed_kernel(
-    n2_ref, dy_ref, wu_ref, wd_ref, bu_ref, red_ref, dn2_ref, gu_ref, gd_ref, dbu_ref, n2_turned
-):
-    step = pl.program_id(0)
-
-    @pl.when(step == 0)
-    def _():
-        n2_turned[...] = n2_ref[...].T
-        red_ref[...] = jnp.zeros_like(red_ref)
-        dn2_ref[...] = jnp.zeros_like(dn2_ref)
-
-    normed = n2_ref[...]
-    grad_top = dy_ref[...]
-    expanded = dot_nn(normed, wu_ref[...]) + bu_ref[...]
-    phi = 0.5 + 0.5 * lax.erf(expanded * (0.5**0.5))
-    density = jnp.exp(-0.5 * expanded * expanded) * 0.3989422804014327
-    hidden = (expanded * phi).astype(low)
-    slope = phi + expanded * density
-    grad_hidden = dot_nt(grad_top, wd_ref[...])
-    grad_expanded = grad_hidden * slope
-    grad_low = grad_expanded.astype(low)
-    red_ref[...] += dot_nn(hidden, wd_ref[...])
-    dn2_ref[...] += dot_nt(grad_low, wu_ref[...])
-    gu_ref[...] = dot_nn(n2_turned[...], grad_low).astype(low)
-    gd_ref[...] = dot_tn(hidden, grad_top).astype(low)
-    dbu_ref[...] = jnp.sum(grad_low.astype(jnp.float32), axis=0, keepdims=True)
-
-
-def feed_both(normed, grad_top, expand_low, reduce_low, expand_bias):
-    rows, features = normed.shape
-    hidden_count = reduce_low.shape[0]
-    block = 512
-    whole = pl.BlockSpec((rows, features), lambda j: (0, 0))
-    across = pl.BlockSpec((features, block), lambda j: (0, j))
-    down = pl.BlockSpec((block, features), lambda j: (j, 0))
-    bias = pl.BlockSpec((1, block), lambda j: (0, j))
-    return pl.pallas_call(
-        feed_kernel,
-        grid=(hidden_count // block,),
-        in_specs=[whole, whole, across, down, bias],
-        out_specs=[whole, whole, across, down, bias],
-        out_shape=[
-            jax.ShapeDtypeStruct((rows, features), jnp.float32),
-            jax.ShapeDtypeStruct((rows, features), jnp.float32),
-            jax.ShapeDtypeStruct((features, hidden_count), low),
-            jax.ShapeDtypeStruct((hidden_count, features), low),
-            jax.ShapeDtypeStruct((1, hidden_count), jnp.float32),
-        ],
-        scratch_shapes=[pltpu.VMEM((features, rows), low)],
+def feed_kernel(block_parts, has_sums, *refs):
+    refs = list(refs)
+    take = lambda count: [refs.pop(0) for _ in range(count)]
+    normed = [ref[...] for ref in take(2)]
+    tops = [ref[...] for ref in take(2)]
+    blocks = [(take(parts), take(parts), take(1)[0]) for parts in block_parts]
+    earlier = take(4) if has_sums else None
+    reduced = take(2)
+    grad_normed = take(2)
+    outs = [(take(2), take(2), take(1)[0]) for _ in block_parts]
+    turned = take(1)[0]
+    rows = normed[0].shape[0]
+    for side in range(2):
+        turned[:, side * rows : (side + 1) * rows] = normed[side].T
+        if has_sums:
+            reduced[side][...] = earlier[side][...]
+            grad_normed[side][...] = earlier[2 + side][...]
+    for index, ((wu_parts, wd_parts, bias), (gu_refs, gd_refs, dbu_ref)) in enumerate(
+        zip(blocks, outs)
+    ):
+        expand = jnp.concatenate([ref[...] for ref in wu_parts], axis=0)
+        reduce = jnp.concatenate([ref[...] for ref in wd_parts], axis=0)
+        hiddens, grads = [], []
+        for side in range(2):
+            expanded = dot_nn(normed[side], expand) + bias[...]
+            phi = 0.5 + 0.5 * lax.erf(expanded * (0.5**0.5))
+            density = jnp.exp(-0.5 * expanded * expanded) * 0.3989422804014327
+            hidden = (expanded * phi).astype(low)
+            slope = phi + expanded * density
+            grad_low = (dot_nt(tops[side], reduce) * slope).astype(low)
+            down = dot_nn(hidden, reduce)
+            back = dot_nt(grad_low, expand)
+            if has_sums or index:
+                reduced[side][...] += down
+                grad_normed[side][...] += back
+            else:
+                reduced[side][...] = down
+                grad_normed[side][...] = back
+            hiddens.append(hidden)
+            grads.append(grad_low)
+        grad_both = jnp.concatenate(grads, axis=0)
+        half = gu_refs[0].shape[0]
+        for part in range(2):
+            gu_refs[part][...] = dot_nn(
+                turned[part * half : (part + 1) * half, :], grad_both
+            ).astype(low)
+        grad_reduce = sum(dot_tn(hiddens[side], tops[side]) for side in range(2)).astype(low)
+        half = gd_refs[0].shape[0]
+        for part in range(2):
+            gd_refs[part][...] = grad_reduce[part * half : (part + 1) * half]
+        dbu_ref[...] = jnp.sum(grad_both.astype(jnp.float32), axis=0, keepdims=True)
+
+
+def feed_blocks(normed, tops, blocks, sums):
+    rows, features = normed[0].shape
+    units = blocks[0][1][0].shape[-2] * len(blocks[0][1])
+    operands = [*normed, *tops]
+    for wu_parts, wd_parts, bias in blocks:
+        operands += [*wu_parts, *wd_parts, bias]
+    sum_shape = jax.ShapeDtypeStruct((rows, features), jnp.float32)
+    shapes = [sum_shape] * 4
+    for _ in blocks:
+        shapes += [jax.ShapeDtypeStruct((features // 2, units), low)] * 2
+        shapes += [jax.ShapeDtypeStruct((units // 2, features), low)] * 2
+        shapes += [jax.ShapeDtypeStruct((1, units), jnp.float32)]
+    if sums is not None:
+        operands += list(sums)
+    in_vmem = pl.BlockSpec(memory_space=pltpu.VMEM)
+    results = pl.pallas_call(
+        partial(feed_kernel, [len(block[0]) for block in blocks], sums is not None),
+        in_specs=[in_vmem] * len(operands),
+        out_specs=[in_vmem] * len(shapes),
+        out_shape=shapes,
+        scratch_shapes=[pltpu.VMEM((features, 2 * rows), low)],
         compiler_params=pltpu.CompilerParams(vmem_limit_bytes=vmem_bytes),
         cost_estimate=pl.CostEstimate(
-            flops=12 * rows * features * hidden_count,
-            bytes_accessed=8 * features * hidden_count,
-            transcendentals=2 * rows * hidden_count,
+            flops=24 * rows * features * units * len(blocks),
+            bytes_accessed=8 * features * units * len(blocks),
+            transcendentals=4 * rows * units * len(blocks),
         ),
-        name="feed_both",
-    )(normed, grad_top, expand_low, reduce_low, expand_bias)
+        name="feed_blocks",
+    )(*operands)
+    grads = [results[4 + 5 * index : 9 + 5 * index] for index in range(len(blocks))]
+    return results[:4], grads
 
 
 def chip_routes(dp_count, seq_count):
@@ -325,16 +352,27 @@
     vector_second,
 ):
     axes = ("dp", "seq")
-    everyone = ("seq", "dp")
     dp_index = lax.axis_index("dp")
     seq_index = lax.axis_index("seq")
     core = dp_index % 2
+    group = dp_index // 2
+    groups = dp_count // 2
+    four_chips = groups == 4
     odd = seq_index % 2
     features = activations.shape[2]
     quarter = activations.shape[1]
+    half = features // 2
+    owned = inputs_weight.shape[0]
+    owned_units = reduce_weight.shape[0]
+    rows_piece = owned // groups
+    units_piece = owned_units // dp_count
     vector_rows = vector_params.shape[0]
     straight, crossed = chip_routes(dp_count, seq_count)
     core_pairs = [(place, place ^ 1) for place in range(dp_count)]
+    x_pairs = [(place, place ^ 2) for place in range(dp_count)]
+    y_pairs = [(place, place ^ 4) for place in range(dp_count)]
+    far_pairs = [(place, place ^ 6) for place in range(dp_count)]
+    same_core = [list(range(first, dp_count, 2)) for first in range(2)]
 
     def to_chip(values):
         near = lax.dynamic_index_in_dim(values, odd, 0, keepdims=False)
@@ -355,74 +393,218 @@
     def swap_cores(values):
         return lax.ppermute(values, "dp", core_pairs)
 
-    def own_piece(weight):
-        rows = weight.shape[0] // dp_count
-        return lax.dynamic_slice_in_dim(weight, dp_index * rows, rows, 0).astype(low)
-
-    def spread(piece):
-        return lax.all_gather(piece, everyone, axis=0, tiled=True)
-
-    vector_piece = jnp.pad(own_piece(vector_params.T), ((0, 0), (0, LANES - vector_rows)))
-    first_low = spread(
-        jnp.concatenate([own_piece(inputs_weight), own_piece(output_weight), vector_piece], axis=1)
-    )
-    expand_low = spread(own_piece(expand_weight))
-    reduce_low = spread(own_piece(reduce_weight))
-    wide = 3 * features
-    inputs_low = first_low[:, :wide]
-    output_low = first_low[:, wide : wide + features]
-    vectors = first_low[:, wide + features : wide + features + vector_rows].T.astype(jnp.float32)
+    def via_x(values):
+        return lax.ppermute(values, "dp", x_pairs)
+
+    def via_y(values):
+        return lax.ppermute(values, "dp", y_pairs)
+
+    def by_core(mine, theirs, axis):
+        return jnp.where(
+            core == 0,
+            jnp.concatenate([mine, theirs], axis=axis),
+            jnp.concatenate([theirs, mine], axis=axis),
+        )
+
+    def add_low(*terms):
+        return sum(term.astype(jnp.float32) for term in terms).astype(low)
+
+    def gather_z(piece):
+        return lax.all_gather(piece, "seq", axis=0, tiled=False)
+
+    def gather_chips(block):
+        middle = block.shape[0] // 2
+        from_x = via_x(block)
+        from_y = via_y(block)
+        return block, from_x, from_y, via_y(from_x[:middle]), via_x(from_y[middle:])
+
+    def in_order(own, from_x, from_y, from_far, axis):
+        x_set = group % 2 == 1
+        y_set = group // 2 == 1
+        near_low = jnp.where(x_set, from_x, own)
+        near_high = jnp.where(x_set, own, from_x)
+        far_low = jnp.where(x_set, from_far, from_y)
+        far_high = jnp.where(x_set, from_y, from_far)
+        return jnp.stack(
+            [
+                jnp.where(y_set, far_low, near_low),
+                jnp.where(y_set, far_high, near_high),
+                jnp.where(y_set, near_low, far_low),
+                jnp.where(y_set, near_high, far_high),
+            ],
+            axis=axis,
+        )
+
+    def scatter_chips(own, to_x, to_y, to_far):
+        y_first = add_low(to_y[0], via_x(to_far[0]))
+        x_second = add_low(to_x[1], via_y(to_far[1]))
+        x_first, y_second = via_x(to_x[0]), via_y(to_y[1])
+        first = add_low(own[0], x_first, via_y(y_first))
+        second = add_low(own[1], via_x(x_second), y_second)
+        return jnp.concatenate([first, second], axis=0)
+
+    def scatter_z(blocks):
+        total = lax.dynamic_index_in_dim(blocks, seq_index, 0, keepdims=False)
+        total = total.astype(jnp.float32)
+        for shift in range(1, seq_count):
+            target = (seq_index + shift) % seq_count
+            sent = lax.dynamic_index_in_dim(blocks, target, 0, keepdims=False)
+            ring = [(place, (place + shift) % seq_count) for place in range(seq_count)]
+            total = total + lax.ppermute(sent, "seq", ring).astype(jnp.float32)
+        return total.astype(low)
+
+    def regather(piece):
+        if not four_chips:
+            every = lax.all_gather(piece, "dp", axis=0, tiled=False)
+            return every.reshape((groups, 2) + piece.shape)
+        from_far = lax.ppermute(piece, "dp", far_pairs)
+        mine = in_order(piece, via_x(piece), via_y(piece), from_far, 0)
+        return by_core(mine[:, None], swap_cores(mine)[:, None], 1)
+
+    def corner(weight, column):
+        return lax.dynamic_slice(
+            weight, (group * rows_piece, column + core * half), (rows_piece, half)
+        ).astype(low)
+
+    vector_piece = lax.dynamic_slice_in_dim(vector_params, group * rows_piece, rows_piece, 1)
+    first_piece = jnp.concatenate(
+        [
+            corner(inputs_weight, 0),
+            corner(inputs_weight, features),
+            corner(inputs_weight, 2 * features),
+            corner(output_weight, 0),
+            jnp.pad(vector_piece.T.astype(low), ((0, 0), (0, LANES - vector_rows))),
+        ],
+        axis=1,
+    )
+    expand_piece = jnp.concatenate(
+        [
+            lax.dynamic_slice_in_dim(
+                expand_weight, owner * owned_units + dp_index * units_piece, units_piece, 1
+            ).astype(low)
+            for owner in range(seq_count)
+        ],
+        axis=1,
+    )
+    reduce_piece = lax.dynamic_slice_in_dim(
+        reduce_weight, dp_index * units_piece, units_piece, 0
+    ).astype(low)
 
     residual_low = to_chip(activations)
+    first_block = gather_z(first_piece)
+    expand_block = gather_z(expand_piece)
+    reduce_block = gather_z(reduce_piece)
     grad_top = to_chip(cotangent)
     rows_here = residual_low.shape[0]
+    residual_other = swap_cores(residual_low)
+    grad_top_other = swap_cores(grad_top)
     other_segments = swap_cores(segment_ids)
     segment_pair = jnp.where(seq_index // 2 == core, segment_ids, other_segments)
     segments = lax.dynamic_index_in_dim(segment_pair, odd, 0, keepdims=False)
     seg_row, seg_col = segments[None, :], segments[:, None]
 
-    residual = residual_low.astype(jnp.float32)
-    unit_one, inverse_one = normalize(residual)
-    normed_one = (unit_one * vectors[0] + vectors[1]).astype(low)
-    projected = dot_nn(normed_one, inputs_low)
-    queries = (projected[:, :features] + vectors[4]).astype(low)
-    keys = projected[:, features : 2 * features].astype(low)
-    values = (projected[:, 2 * features :] + vectors[5]).astype(low)
-    half = features // 2
-    group_low = jnp.concatenate([queries[:, :half], keys[:, :half], values[:, :half]], axis=1)
-    group_high = jnp.concatenate([queries[:, half:], keys[:, half:], values[:, half:]], axis=1)
-
-    def join_tokens(mine, theirs):
-        return jnp.where(
-            core == 0,
-            jnp.concatenate([mine, theirs], axis=0),
-            jnp.concatenate([theirs, mine], axis=0),
-        )
+    if four_chips:
+        own, from_x, from_y, far_first, far_second = gather_chips(first_block)
+        from_far = jnp.concatenate([far_first, far_second], axis=0)
+        first_low = in_order(own, from_x, from_y, from_far, 1)
+    else:
+        first_low = lax.all_gather(
+            first_block, "dp", axis=1, tiled=False, axis_index_groups=same_core
+        )
+    first_low = first_low.reshape(features, first_low.shape[-1])
+    wide = 3 * half
+    inputs_low = first_low[:, :wide]
+    output_half = first_low[:, wide : wide + half]
+    output_low = by_core(output_half, swap_cores(output_half), 1)
+    vectors = first_low[:, wide + half : wide + half + vector_rows].T.astype(jnp.float32)
+
+    expand_bias = vectors[8:].reshape(seq_count, dp_count, units_piece)
+    block_units = seq_count * owned_units // 8
+    if four_chips:
+        expand_parts = gather_chips(expand_block.reshape(features, block_units))
+        reduce_parts = gather_chips(reduce_block.reshape(block_units, features))
+        blocks = []
+        for offset in range(4):
+            place = dp_index ^ (2 * offset)
+            bias = lax.dynamic_index_in_dim(expand_bias, place, 1, keepdims=False)
+            picked = slice(offset, offset + 1) if offset < 3 else slice(3, 5)
+            blocks.append(
+                (expand_parts[picked], reduce_parts[picked], bias.reshape(1, block_units))
+            )
+    else:
+        expand_all = lax.all_gather(
+            expand_block.reshape(features, -1), "dp", axis=1, axis_index_groups=same_core
+        ).reshape(features, 4, block_units)
+        reduce_all = lax.all_gather(
+            reduce_block.reshape(-1, features), "dp", axis=0, axis_index_groups=same_core
+        ).reshape(4, block_units, features)
+        picked = lax.dynamic_index_in_dim(
+            expand_bias.reshape(seq_count, groups, 2, units_piece), core, 2, keepdims=False
+        )
+        bias_all = picked.transpose(1, 0, 2).reshape(4, 1, block_units)
+        blocks = [
+            ((expand_all[:, index],), (reduce_all[index],), bias_all[index]) for index in range(4)
+        ]
 
     def tokens_of(values, which):
         return lax.dynamic_slice_in_dim(values, which * rows_here, rows_here, 0)
 
-    mine = jnp.where(core == 0, group_low, group_high)
-    theirs = swap_cores(jnp.where(core == 0, group_high, group_low))
-    projected_heads = join_tokens(mine, theirs)
-    mixture_heads, logs_all = attend_forward(seg_row, seg_col, projected_heads)
-    mixture_mine = tokens_of(mixture_heads, core)
+    def heads_part(vector):
+        return lax.dynamic_slice_in_dim(vector, core * half, half, 0)
+
+    unit_all, _ = normalize(by_core(residual_low, residual_other, 0).astype(jnp.float32))
+    normed_one = (unit_all * vectors[0] + vectors[1]).astype(low)
+    input_bias = jnp.concatenate(
+        [heads_part(vectors[4]), jnp.zeros((half,), jnp.float32), heads_part(vectors[5])]
+    )
+    projected = (dot_nn(normed_one, inputs_low) + input_bias).astype(low)
+    mixture_heads, logs_all = attend_forward(seg_row, seg_col, projected)
     mixture_theirs = swap_cores(tokens_of(mixture_heads, 1 - core))
-    mixture = jnp.where(
-        core == 0,
-        jnp.concatenate([mixture_mine, mixture_theirs], axis=1),
-        jnp.concatenate([mixture_theirs, mixture_mine], axis=1),
-    )
-
+    mixture = by_core(tokens_of(mixture_heads, core), mixture_theirs, 1)
+
+    residual = residual_low.astype(jnp.float32)
     middle = residual + (dot_nn(mixture, output_low) + vectors[6])
     unit_two, inverse_two = normalize(middle)
     normed_two = (unit_two * vectors[2] + vectors[3]).astype(low)
-    reduced, grad_normed_two, grad_expand, grad_reduce, bias_sums = feed_both(
-        normed_two, grad_top, expand_low, reduce_low, vectors[8:].reshape(1, -1)
-    )
+    normed_pair = (normed_two, swap_cores(normed_two))
+    top_pair = (grad_top, grad_top_other)
+    sums, grads = feed_blocks(normed_pair, top_pair, blocks[:3], None)
+    sums, last_grads = feed_blocks(normed_pair, top_pair, blocks[3:], sums)
+    grads = grads + last_grads
+    reduced = sums[0] + swap_cores(sums[1])
+    grad_normed_two = sums[2] + swap_cores(sums[3])
     layer_output = from_chip((middle + (reduced + vectors[7])).astype(low))
-    expand_part = lax.psum_scatter(grad_expand, everyone, scatter_dimension=0, tiled=True)
-    reduce_part = lax.psum_scatter(grad_reduce, everyone, scatter_dimension=0, tiled=True)
+
+    if four_chips:
+        expand_sum = scatter_chips(*[(grad[0], grad[1]) for grad in grads])
+        reduce_sum = scatter_chips(*[(grad[2], grad[3]) for grad in grads])
+        place = jnp.arange(dp_count)[None, :, None]
+        bias_sums = sum(
+            jnp.where(
+                place == (dp_index ^ (2 * offset)),
+                grads[offset][4].reshape(seq_count, 1, units_piece),
+                0.0,
+            )
+            for offset in range(4)
+        )
+    else:
+        expand_sum = jnp.concatenate(
+            [jnp.concatenate([grad[0], grad[1]], axis=0) for grad in grads], axis=1
+        )
+        expand_sum = expand_sum.reshape(features, groups, -1).transpose(1, 0, 2)
+        expand_sum = lax.psum_scatter(expand_sum, "dp", axis_index_groups=same_core)
+        reduce_sum = jnp.concatenate([part for grad in grads for part in grad[2:4]], axis=0)
+        reduce_sum = reduce_sum.reshape(groups, -1, features)
+        reduce_sum = lax.psum_scatter(reduce_sum, "dp", axis_index_groups=same_core)
+        bias_sums = jnp.concatenate([grad[4] for grad in grads], axis=1)
+        bias_sums = bias_sums.reshape(groups, seq_count, units_piece).transpose(1, 0, 2)
+        is_core = jnp.arange(2)[None, None, :, None] == core
+        bias_sums = jnp.where(is_core, bias_sums[:, :, None, :], 0.0)
+    sum_expand = regather(scatter_z(expand_sum.reshape(seq_count, owned, -1)))
+    sum_reduce = regather(scatter_z(reduce_sum.reshape(seq_count, units_piece, features)))
+    sum_expand = sum_expand.reshape(dp_count, owned, seq_count, units_piece)
+    sum_expand = sum_expand.transpose(1, 2, 0, 3).reshape(expand_weight.shape)
+    sum_reduce = sum_reduce.reshape(reduce_weight.shape)
 
     grad_middle = grad_top.astype(jnp.float32) + norm_back(
         grad_normed_two, vectors[2], unit_two, inverse_two
@@ -430,28 +612,35 @@
     grad_attended = grad_middle.astype(low)
     grad_output = dot_tn(mixture, grad_attended).astype(low)
     grad_mixture = dot_nt(grad_attended, output_low).astype(low)
-    grad_mine = jnp.where(core == 0, grad_mixture[:, :half], grad_mixture[:, half:])
-    grad_theirs = swap_cores(jnp.where(core == 0, grad_mixture[:, half:], grad_mixture[:, :half]))
+
+    def columns_of(values, which):
+        return lax.dynamic_slice_in_dim(values, which * half, half, 1)
+
+    grad_theirs = swap_cores(columns_of(grad_mixture, 1 - core))
     grad_heads = attend_backward(
-        seg_row, seg_col, projected_heads, logs_all, join_tokens(grad_mine, grad_theirs)
-    )
-    grad_all = jnp.concatenate(grad_heads, axis=1)
-    back_mine = tokens_of(grad_all, core)
-    back_theirs = swap_cores(tokens_of(grad_all, 1 - core))
-    back_low = jnp.where(core == 0, back_mine, back_theirs)
-    back_high = jnp.where(core == 0, back_theirs, back_mine)
-    grad_projected = jnp.concatenate(
-        [
-            part[:, start : start + half]
-            for start in (0, half, 2 * half)
-            for part in (back_low, back_high)
-        ],
-        axis=1,
-    )
+        seg_row,
+        seg_col,
+        projected,
+        logs_all,
+        by_core(columns_of(grad_mixture, core), grad_theirs, 0),
+    )
+    output_sum = add_low(
+        columns_of(grad_output, core), swap_cores(columns_of(grad_output, 1 - core))
+    )
+    grad_projected = jnp.concatenate(grad_heads, axis=1)
     grad_inputs = dot_tn(normed_one, grad_projected).astype(low)
-    grad_normed_one = dot_nt(grad_projected, inputs_low)
+    grad_normed_all = dot_nt(grad_projected, inputs_low)
+    grad_normed_one = tokens_of(grad_normed_all, core) + swap_cores(
+        tokens_of(grad_normed_all, 1 - core)
+    )
+    unit_one, inverse_one = normalize(residual)
     grad_residual = norm_back(grad_normed_one, vectors[0], unit_one, inverse_one)
     input_grad = from_chip((grad_middle + grad_residual).astype(low))
+
+    def heads_sum(values):
+        return lax.dynamic_update_slice_in_dim(
+            jnp.zeros((features,), jnp.float32), column_sum(values), core * half, 0
+        )
 
     head_rows = jnp.stack(
         [
@@ -459,44 +648,43 @@
             column_sum(grad_normed_one),
             column_sum(grad_normed_two * unit_two),
             column_sum(grad_normed_two),
-            column_sum(grad_projected[:, :features]),
-            column_sum(grad_projected[:, 2 * features :]),
+            heads_sum(grad_heads[0]),
+            heads_sum(grad_heads[2]),
             column_sum(grad_attended),
             column_sum(grad_top),
         ]
     )
     grad_vectors = jnp.concatenate([head_rows, bias_sums.reshape(-1, features)], axis=0)
     vector_columns = jnp.pad(grad_vectors.T.astype(low), ((0, 0), (0, LANES - vector_rows)))
-    first_part = lax.psum_scatter(
-        jnp.concatenate([grad_inputs, grad_output, vector_columns], axis=1),
-        everyone,
-        scatter_dimension=0,
-        tiled=True,
-    )
-
-    def regather(part):
-        return lax.all_gather(part, "dp", axis=0, tiled=True).astype(jnp.float32)
-
-    sum_expand = regather(expand_part)
-    sum_reduce = regather(reduce_part)
-    sum_first = regather(first_part)
-    sum_inputs = sum_first[:, :wide]
-    sum_output = sum_first[:, wide : wide + features]
-    sum_vectors = sum_first[:, wide + features : wide + features + vector_rows].T
-
-    new_inputs = adamw_step(
-        inputs_weight, inputs_moment, inputs_second, sum_inputs, 0.03, decay_rate
-    )
-    new_output = adamw_step(
-        output_weight, output_moment, output_second, sum_output, 0.3, decay_rate
-    )
-    new_expand = adamw_step(
-        expand_weight, expand_moment, expand_second, sum_expand, 0.03, decay_rate
-    )
-    new_reduce = adamw_step(
-        reduce_weight, reduce_moment, reduce_second, sum_reduce, 0.02, decay_rate
-    )
-    new_vectors = adamw_step(vector_params, vector_moment, vector_second, sum_vectors, 0.5, 0.0)
+    first_grad = jnp.concatenate([grad_inputs, output_sum, vector_columns], axis=1)
+    first_grad = first_grad.reshape(seq_count, groups, rows_piece, -1)
+    if four_chips:
+        split = []
+        for offset in range(4):
+            block = lax.dynamic_index_in_dim(first_grad, group ^ offset, 1, keepdims=False)
+            split.append((block[: seq_count // 2], block[seq_count // 2 :]))
+        first_sum = scatter_chips(*split)
+    else:
+        first_sum = lax.psum_scatter(
+            first_grad, "dp", scatter_dimension=1, axis_index_groups=same_core
+        )
+    sum_first = regather(scatter_z(first_sum)).transpose(0, 2, 1, 3)
+    sum_inputs = sum_first[..., :wide].reshape(groups, rows_piece, 2, 3, half)
+    sum_inputs = sum_inputs.transpose(0, 1, 3, 2, 4).reshape(inputs_weight.shape)
+    sum_output = sum_first[..., wide : wide + half].reshape(output_weight.shape)
+    sum_vectors = sum_first[..., wide + half : wide + half + vector_rows].astype(jnp.float32)
+    sum_vectors = jnp.sum(sum_vectors, axis=2).reshape(owned, vector_rows).T
+
+    def renew(weight, moment, second, gradient, step_rate, weight_decay):
+        return adamw_step(
+            weight, moment, second, gradient.astype(jnp.float32), step_rate, weight_decay
+        )
+
+    new_inputs = renew(inputs_weight, inputs_moment, inputs_second, sum_inputs, 0.03, decay_rate)
+    new_output = renew(output_weight, output_moment, output_second, sum_output, 0.3, decay_rate)
+    new_expand = renew(expand_weight, expand_moment, expand_second, sum_expand, 0.03, decay_rate)
+    new_reduce = renew(reduce_weight, reduce_moment, reduce_second, sum_reduce, 0.02, decay_rate)
+    new_vectors = renew(vector_params, vector_moment, vector_second, sum_vectors, 0.5, 0.0)
     return (
         layer_output,
         input_grad,

time: 686 us -> 443 us (0.65)
  waiting for transfers between devices: 464 us -> 99.9 us
  starting transfers between devices: 22.3 us -> 97.5 us
  blocking collectives: 0 us -> 54.1 us
  between operations: 15 us -> 2.53 us
  Pallas kernels: 43.9 us -> 54.3 us
    all_gather x6 -> x0, waiting for transfers between devices: 192 us -> none  [the longest x3 128 us: spread(): return lax.all_gather(piece, everyone, axis=0, tiled=True)]
    reduce_scatter x2 -> x0, waiting for transfers between devices: 161 us -> none  [the longest x1 112 us: on_device(): lax.psum_scatter(grad_expand, everyone, scatter_dimension=0, tiled=True)]
    ppermute x0 -> x48, waiting for transfers between devices: none -> 83.5 us  [the longest x9 37.6 us: scatter_z(): total = total + lax.ppermute(sent, 'seq', ring).astype(jnp.float32)]
    unnamed x10 -> x0, waiting for transfers between devices: 60.4 us -> none
    all_gather x0 -> x3, blocking collectives: none -> 54.1 us  [gather_z(): return lax.all_gather(piece, 'seq', axis=0, tiled=False)]
    ppermute x0 -> x48, starting transfers between devices: none -> 47 us  [the longest x18 17.8 us: via_x(): return lax.ppermute(values, 'dp', x_pairs)]
    unnamed x111 -> x166, local copies, waits for them, and re-layouts: 36.5 us -> 13.6 us
    ppermute x5 -> x14, starting transfers between devices: 2.75 us -> 24 us  [swap_cores(): return lax.ppermute(values, 'dp', core_pairs)]
  transfers between devices with their start and end apart: 22 -> 70, of which waited for: 15 -> 24; matrix products, arithmetic and copies ran while one was open for 14% -> 22% of each run, Pallas kernels for 4% -> 10%
where the time goes in v2:
time: 443 us; the launch traced here: 434 us
  waiting for transfers between devices  99.9 us (23%)
  starting transfers between devices  97.5 us (22%)
  local copies, waits for them, and re-layouts  61 us (14%)
  Pallas kernels  54.3 us (12%)
  blocking collectives  54.1 us (12%)
  other arithmetic  52.1 us (12%)
  matrix products  12.7 us (3%)
    all_gather x3, blocking collectives, gather_z(): return lax.all_gather(piece, 'seq', axis=0, tiled=False)  54.1 us
    ppermute x9, waiting for transfers between devices, scatter_z(): total = total + lax.ppermute(sent, 'seq', ring).astype(jnp.float32)  37.6 us
    pallas_call x2, Pallas kernels, feed_blocks(): pl.pallas_call(partial(feed_kernel, [len(block[0]) for block in blocks],...  29.6 us
    ppermute x14, starting transfers between devices, swap_cores(): return lax.ppermute(values, 'dp', core_pairs)  24 us
    ppermute x18, waiting for transfers between devices, via_x(): return lax.ppermute(values, 'dp', x_pairs)  22.7 us
    convert_element_type x8, local copies, waits for them, and re-layouts, renew(): gradient.astype(jnp.float32)  20.1 us
    ppermute x18, waiting for transfers between devices, via_y(): return lax.ppermute(values, 'dp', y_pairs)  19.8 us
    ppermute x18, starting transfers between devices, via_x(): return lax.ppermute(values, 'dp', x_pairs)  17.8 us
  transfers between devices with their start and end apart: 70, of which 24 were waited for; matrix products, arithmetic and copies ran while one was open for 22% of the time, Pallas kernels for 10%

profile of v2, /device:TPU:9, one launch (start us, length us, event | category | flops | bytes accessed | tf_op | source)
XLA Modules:
  0.0 434.2 jit_solution(14368863718932030379)
XLA Ops:
  5.3 13.4 %all-gather = bf16[192,1664]{1,0:T(8,128)(2,1)S(1)} all-gather(bf16[48,1664]{1,0:T(8,128)(2,1)S(1)} %constant_dynamic-update-slice_fusion), channel_id=2, replica_groups=mesh['dp'=8,'seq'=4] {'seq'}, dimensions={0}, use_global_device_ids=true | all-gather | bytes 798720 | tf_op jit(solution)/shard_map/all_gather | solution.py:413
  21.1 5.0 %collective-permute-start.2 = (s32[2,1024]{1,0:T(2,128)}, s32[2,1024]{1,0:T(2,128)S(1)}, u32[]{:S(2)}, u32[]{:S(2)}) collective-permute-start(s32[2,1024]{1,0:T(2,128)} %param.20), channel_id=1, source_target_pairs={{0,4},{4,0},{8,12},{12,8},{16,20},{20,16},{24,28},{28,24},{1,5},{5... | collective-permute-start | bytes 24584 | tf_op jit(solution)/shard_map/ppermute | solution.py:394
  27.1 4.1 collective-permute-start
  32.9 25.7 %all-gather.1.refs_4_ = bf16[768,384]{1,0:T(8,128)(2,1)} all-gather(bf16[192,384]{1,0:T(8,128)(2,1)S(1)} %pad_maximum_fusion.10), channel_id=3, replica_groups=mesh['dp'=8,'seq'=4] {'seq'}, dimensions={0}, use_global_device_ids=true | all-gather | bytes 737280 | tf_op jit(solution)/shard_map/all_gather | solution.py:413
  59.6 15.0 %all-gather.2.refs_5_ = bf16[384,768]{1,0:T(8,128)(2,1)} all-gather(bf16[96,768]{1,0:T(8,128)(2,1)S(1)} %dynamic-slice_convert_fusion), channel_id=4, replica_groups=mesh['dp'=8,'seq'=4] {'seq'}, dimensions={0}, use_global_device_ids=true | all-gather | bytes 737280 | tf_op jit(solution)/shard_map/all_gather | solution.py:413
  77.7 10.2 %collective-permute-start.11 = (bf16[256,768]{1,0:T(8,128)(2,1)}, bf16[256,768]{1,0:T(8,128)(2,1)S(1)}, u32[]{:S(2)}, u32[]{:S(2)}) collective-permute-start(bf16[256,768]{1,0:T(8,128)(2,1)} %get-tuple-element.149), channel_id=1, source_target_pairs={{0,0},{1,1},{2,4},{3,5},{4,2},{5,3},{6,6},{7,7},{8,8},{9,9},{10,12... | collective-permute-start | bytes 1179656 | tf_op jit(solution)/shard_map/ppermute | solution.py:380
  91.8 5.8 %collective-permute-done.5 = bf16[2,48,1664]{2,1,0:T(8,128)(2,1)S(1)} collective-permute-done((bf16[2,48,1664]{2,1,0:T(8,128)(2,1)S(1)}, bf16[2,48,1664]{2,1,0:T(8,128)(2,1)S(1)}, u32[]{:S(2)}, u32[]{:S(2)}) %collective-permute-start.5) | collective-permute-done | bytes 319520 | tf_op jit(solution)/shard_map/ppermute | solution.py:400
  97.7 4.7 %collective-permute-start.12 = (bf16[256,768]{1,0:T(8,128)(2,1)S(1)}, bf16[256,768]{1,0:T(8,128)(2,1)S(1)}, u32[]{:S(2)}, u32[]{:S(2)}) collective-permute-start(bf16[256,768]{1,0:T(8,128)(2,1)S(1)} %copy-done.30), channel_id=1, source_target_pairs={{0,1},{1,0},{2,5},{3,4},{4,3},{5,2},{6,7},{7,6},{8,9},{9,8},{10,13... | collective-permute-start | bytes 1179656 | tf_op jit(solution)/shard_map/ppermute | solution.py:381
  108.4 4.0 add_convert_fusion.q_ref.k_ref.v_ref
  112.4 9.4 %attend_forward.1 = (bf16[1024,384]{1,0:T(8,128)(2,1)}, f32[3,8,1024]{2,1,0:T(8,128)}) custom-call(s32[1,1024]{1,0:T(1,128)} %copy-done.38, s32[1024,1]{1,0:T(8,128)} %copy.106.seg_col, bf16[1024,1152]{1,0:T(8,128)(2,1)} %add_convert_fusion.q_ref.k_ref.v_ref, bf16[1024,1152]{1,0:T(8,128)(2,1)} %add_convert_fusion.q_ref.k_ref.v_ref, ...), custom_call_target="tpu_custom_call" | custom-call | flops 1610612736 | bytes 3145728 | tf_op jit(solution)/shard_map/attend_forward/pallas_call | solution.py:177
  151.5 19.4 %feed_blocks.2 = (f32[512,768]{1,0:T(8,128)}, f32[512,768]{1,0:T(8,128)}, f32[512,768]{1,0:T(8,128)}, f32[512,768]{1,0:T(8,128)}, bf16[384,384]{1,0:T(8,128)(2,1...) custom-call(bf16[512,768]{1,0:T(8,128)(2,1)} %add_convert_fusion.2.r, ...), custom_call_target="tpu_custom_call" | custom-call | flops 10871635968 | bytes 7077888 | tf_op jit(solution)/shard_map/feed_blocks/pallas_call | solution.py:302
  171.7 10.2 %feed_blocks.3 = (f32[512,768]{1,0:T(8,128)}, f32[512,768]{1,0:T(8,128)}, f32[512,768]{1,0:T(8,128)}, f32[512,768]{1,0:T(8,128)}, bf16[384,384]{1,0:T(8,128)(2,1...) custom-call(bf16[512,768]{1,0:T(8,128)(2,1)} %add_convert_fusion.2.refs_0_, ...), custom_call_target="tpu_custom_call" | custom-call | flops 3623878656 | bytes 2359296 | tf_op jit(solution)/shard_map/feed_blocks/pallas_call | solution.py:302
  192.7 4.0 collective-permute-done.45
  199.0 4.6 %collective-permute-done.60 = bf16[192,768]{1,0:T(8,128)(2,1)S(1)} collective-permute-done((bf16[192,768]{1,0:T(8,128)(2,1)}, bf16[192,768]{1,0:T(8,128)(2,1)S(1)}, u32[]{:S(2)}, u32[]{:S(2)}) %collective-permute-start.60) | collective-permute-done | bytes 294944 | tf_op jit(solution)/shard_map/ppermute | solution.py:400
  204.9 4.5 %collective-permute-done.58 = bf16[192,768]{1,0:T(8,128)(2,1)S(1)} collective-permute-done((bf16[192,768]{1,0:T(8,128)(2,1)}, bf16[192,768]{1,0:T(8,128)(2,1)S(1)}, u32[]{:S(2)}, u32[]{:S(2)}) %collective-permute-start.58) | collective-permute-done | bytes 294944 | tf_op jit(solution)/shard_map/ppermute | solution.py:397
  211.0 4.7 %collective-permute-done.48 = bf16[384,384]{1,0:T(8,128)(2,1)S(1)} collective-permute-done((bf16[384,384]{1,0:T(8,128)(2,1)S(1)}, bf16[384,384]{1,0:T(8,128)(2,1)S(1)}, u32[]{:S(2)}, u32[]{:S(2)}) %collective-permute-start.48) | collective-permute-done | bytes 294944 | tf_op jit(solution)/shard_map/ppermute | solution.py:397
  222.4 5.1 %collective-permute-start.22 = (f32[512,768]{1,0:T(8,128)S(1)}, f32[512,768]{1,0:T(8,128)S(1)}, u32[]{:S(2)}, u32[]{:S(2)}) collective-permute-start(f32[512,768]{1,0:T(8,128)S(1)} %copy-done.68), channel_id=1, source_target_pairs={{0,4},{4,0},{8,12},{12,8},{16,20},{20,16},{24,28},{28,24},{1,5},{5... | collective-permute-start | bytes 4718600 | tf_op jit(solution)/shard_map/ppermute | solution.py:394
  234.0 4.2 collective-permute-done.51
  241.8 4.9 %collective-permute-done.50 = bf16[192,384]{1,0:T(8,128)(2,1)S(1)} collective-permute-done((bf16[192,384]{1,0:T(8,128)(2,1)S(1)}, bf16[192,384]{1,0:T(8,128)(2,1)S(1)}, u32[]{:S(2)}, u32[]{:S(2)}) %collective-permute-start.50) | collective-permute-done | bytes 147488 | tf_op jit(solution)/shard_map/ppermute | solution.py:453
  259.5 8.8 %collective-permute-start.56 = (bf16[4,192,384]{2,1,0:T(8,128)(2,1)S(1)}, bf16[4,192,384]{2,1,0:T(8,128)(2,1)S(1)}, u32[]{:S(2)}, u32[]{:S(2)}) collective-permute-start(bf16[4,192,384]{2,1,0:T(8,128)(2,1)S(1)} %get-tuple-element.176), channel_id=1, source_target_pairs={{0,4},{4,0},{8,12},{12,8},{16,20},{20,16},{24,28},{28,24},{1,5},{5... | collective-permute-start | bytes 1769480 | tf_op jit(solution)/shard_map/ppermute | solution.py:394
  268.3 3.9 multiply_reduce_fusion
  280.3 5.4 %copy.117 = f32[192,4,8,96]{3,2,1,0:T(8,128)} copy(f32[192,4,8,96]{3,1,0,2:T(4,128)} %bitcast.192) | data formatting | bytes 4718592 | tf_op jit(solution)/shard_map/convert_element_type | solution.py:680
  291.4 15.3 %attend_backward.1 = (bf16[1024,384]{1,0:T(8,128)(2,1)}, bf16[1024,384]{1,0:T(8,128)(2,1)}, bf16[1024,384]{1,0:T(8,128)(2,1)}) custom-call(s32[1,1024]{1,0:T(1,128)} %copy-done.38, s32[1024,1]{1,0:T(8,128)} %copy.106.seg_col, bf16[1024,1152]{1,0:T(8,128)(2,1)} %add_convert_fusion.q_ref.k_ref.v_ref, bf16[1024,1152]{1,0:T(8,128)(2,1)} %add_convert_fusion.q_ref.k_ref.v_ref, ...), custom_call_target="tpu_custom_call" | custom-call | flops 4026531840 | bytes 5505024 | tf_op jit(solution)/shard_map/attend_backward/pallas_call | solution.py:206
  326.9 4.3 multiply_subtract_fusion.1
  335.3 4.4 %multiply_subtract_fusion = (f32[768,768]{1,0:T(8,128)}, f32[768,768]{1,0:T(8,128)}, f32[768,768]{1,0:T(8,128)}) fusion(f32[768,768]{1,0:T(8,128)S(1)} %copy-done.12, f32[4,2,96,768]{3,2,1,0:T(8,128)S(1)} %copy.118, f32[768,768]{1,0:T(8,128)S(1)} %copy-done.15, f32[768,768]{1,0:T(8,128)S(1)} %copy-done.16), kind=kLoop, calls=%fused_computation.24 | loop fusion | flops 8847360 | bytes 16515072 | tf_op jit(solution)/shard_map/sub | solution.py:79
  342.4 6.7 %collective-permute-done.35 = bf16[2,48,1664]{2,1,0:T(8,128)(2,1)S(1)} collective-permute-done((bf16[2,48,1664]{2,1,0:T(8,128)(2,1)S(1)}, bf16[2,48,1664]{2,1,0:T(8,128)(2,1)S(1)}, u32[]{:S(2)}, u32[]{:S(2)}) %collective-permute-start.35) | collective-permute-done | bytes 319520 | tf_op jit(solution)/shard_map/ppermute | solution.py:397
  350.7 4.5 %collective-permute-start.23 = (bf16[256,768]{1,0:T(8,128)(2,1)S(1)}, bf16[256,768]{1,0:T(8,128)(2,1)S(1)}, u32[]{:S(2)}, u32[]{:S(2)}) collective-permute-start(bf16[256,768]{1,0:T(8,128)(2,1)S(1)} %get-tuple-element.145), channel_id=1, source_target_pairs={{0,0},{1,1},{4,2},{5,3},{2,4},{3,5},{6,6},{7,7},{8,8},{9,9},{12,10... | collective-permute-start | bytes 1179656 | tf_op jit(solution)/shard_map/ppermute | solution.py:389
  360.4 13.3 %collective-permute-done.39 = bf16[48,1664]{1,0:T(8,128)(2,1)S(1)} collective-permute-done((bf16[48,1664]{1,0:T(8,128)(2,1)S(1)}, bf16[48,1664]{1,0:T(8,128)(2,1)S(1)}, u32[]{:S(2)}, u32[]{:S(2)}) %collective-permute-start.39) | collective-permute-done | bytes 159776 | tf_op jit(solution)/shard_map/ppermute | solution.py:453
  373.7 10.9 %collective-permute-done.38 = bf16[48,1664]{1,0:T(8,128)(2,1)S(1)} collective-permute-done((bf16[48,1664]{1,0:T(8,128)(2,1)S(1)}, bf16[48,1664]{1,0:T(8,128)(2,1)S(1)}, u32[]{:S(2)}, u32[]{:S(2)}) %collective-permute-start.38) | collective-permute-done | bytes 159776 | tf_op jit(solution)/shard_map/ppermute | solution.py:453
  398.4 8.8 %collective-permute-done.28 = bf16[256,768]{1,0:T(8,128)(2,1)S(1)} collective-permute-done((bf16[256,768]{1,0:T(8,128)(2,1)S(1)}, bf16[256,768]{1,0:T(8,128)(2,1)S(1)}, u32[]{:S(2)}, u32[]{:S(2)}) %collective-permute-start.28) | collective-permute-done | bytes 393248 | tf_op jit(solution)/shard_map/ppermute | solution.py:389
  407.2 7.5 %collective-permute-done.29 = bf16[256,768]{1,0:T(8,128)(2,1)S(1)} collective-permute-done((bf16[256,768]{1,0:T(8,128)(2,1)S(1)}, bf16[256,768]{1,0:T(8,128)(2,1)S(1)}, u32[]{:S(2)}, u32[]{:S(2)}) %collective-permute-start.29) | collective-permute-done | bytes 393248 | tf_op jit(solution)/shard_map/ppermute | solution.py:390
  425.7 5.9 %multiply_subtract_fusion.2 = (f32[192,2304]{1,0:T(8,128)}, f32[192,2304]{1,0:T(8,128)}, f32[192,2304]{1,0:T(8,128)}) fusion(f32[192,2304]{1,0:T(8,128)} %param.21, f32[192,2304]{1,0:T(8,128)S(1)} %reshape.236, f32[192,2304]{1,0:T(8,128)} %param.22, f32[192,2304]{1,0:T(8,128)} %param.23), kind=kLoop, calls=%fused_computation.33 | loop fusion | flops 6635520 | bytes 12386304 | tf_op jit(solution)/shard_map/sub | solution.py:79
  (444 shorter events, 173.2 us)
Async XLA Ops:
  18.7 58.7 %collective-permute-start.4 = (bf16[4,48,1664]{2,1,0:T(8,128)(2,1)S(1)}, bf16[4,48,1664]{2,1,0:T(8,128)(2,1)S(1)}, u32[]{:S(2)}, u32[]{:S(2)}) collective-permute-start(bf16[4,48,1664]{2,1,0:T(8,128)(2,1)S(1)} %bitcast.202), channel_id=1, source_target_pairs={{0,8},{4,12},{8,0},{12,4},{16,24},{20,28},{24,16},{28,20},{1,9},{5... | collective-permute-start | bytes 1916936 | tf_op jit(solution)/shard_map/ppermute | solution.py:397
  19.9 70.6 %collective-permute-start.6 = (bf16[4,48,1664]{2,1,0:T(8,128)(2,1)S(1)}, bf16[4,48,1664]{2,1,0:T(8,128)(2,1)S(1)}, u32[]{:S(2)}, u32[]{:S(2)}) collective-permute-start(bf16[4,48,1664]{2,1,0:T(8,128)(2,1)S(1)} %bitcast.203), channel_id=1, source_target_pairs={{0,16},{4,20},{8,24},{12,28},{16,0},{20,4},{24,8},{28,12},{1,17},{... | collective-permute-start | bytes 1916936 | tf_op jit(solution)/shard_map/ppermute | solution.py:400
  21.1 54.9 %collective-permute-start.2 = (s32[2,1024]{1,0:T(2,128)}, s32[2,1024]{1,0:T(2,128)S(1)}, u32[]{:S(2)}, u32[]{:S(2)}) collective-permute-start(s32[2,1024]{1,0:T(2,128)} %param.20), channel_id=1, source_target_pairs={{0,4},{4,0},{8,12},{12,8},{16,20},{20,16},{24,28},{28,24},{1,5},{5... | collective-permute-start | bytes 24584 | tf_op jit(solution)/shard_map/ppermute | solution.py:394
  27.1 50.6 %collective-permute-start = (bf16[256,768]{1,0:T(8,128)(2,1)}, bf16[256,768]{1,0:T(8,128)(2,1)S(1)}, u32[]{:S(2)}, u32[]{:S(2)}) collective-permute-start(bf16[256,768]{1,0:T(8,128)(2,1)} %get-tuple-element.155), channel_id=1, source_target_pairs={{0,0},{1,1},{2,4},{3,5},{4,2},{5,3},{6,6},{7,7},{8,8},{9,9},{10,12... | collective-permute-start | bytes 1179656 | tf_op jit(solution)/shard_map/ppermute | solution.py:380
  31.1 56.8 %collective-permute-start.1 = (bf16[256,768]{1,0:T(8,128)(2,1)}, bf16[256,768]{1,0:T(8,128)(2,1)}, u32[]{:S(2)}, u32[]{:S(2)}) collective-permute-start(bf16[256,768]{1,0:T(8,128)(2,1)} %get-tuple-element.156), channel_id=1, source_target_pairs={{0,1},{1,0},{2,5},{3,4},{4,3},{5,2},{6,7},{7,6},{8,9},{9,8},{10,13... | collective-permute-start | bytes 1179656 | tf_op jit(solution)/shard_map/ppermute | solution.py:381
  76.1 54.8 %collective-permute-start.14 = (bf16[768,384]{1,0:T(8,128)(2,1)}, bf16[768,384]{1,0:T(8,128)(2,1)}, u32[]{:S(2)}, u32[]{:S(2)}) collective-permute-start(bf16[768,384]{1,0:T(8,128)(2,1)} %all-gather.1.refs_4_), channel_id=1, source_target_pairs={{0,8},{4,12},{8,0},{12,4},{16,24},{20,28},{24,16},{28,20},{1,9},{5... | collective-permute-start | bytes 1769480 | tf_op jit(solution)/shard_map/ppermute | solution.py:397
  77.4 61.9 %collective-permute-start.16 = (bf16[768,384]{1,0:T(8,128)(2,1)}, bf16[768,384]{1,0:T(8,128)(2,1)}, u32[]{:S(2)}, u32[]{:S(2)}) collective-permute-start(bf16[768,384]{1,0:T(8,128)(2,1)} %all-gather.1.refs_4_), channel_id=1, source_target_pairs={{0,16},{4,20},{8,24},{12,28},{16,0},{20,4},{24,8},{28,12},{1,17},{... | collective-permute-start | bytes 1769480 | tf_op jit(solution)/shard_map/ppermute | solution.py:400
  77.7 45.2 %collective-permute-start.11 = (bf16[256,768]{1,0:T(8,128)(2,1)}, bf16[256,768]{1,0:T(8,128)(2,1)S(1)}, u32[]{:S(2)}, u32[]{:S(2)}) collective-permute-start(bf16[256,768]{1,0:T(8,128)(2,1)} %get-tuple-element.149), channel_id=1, source_target_pairs={{0,0},{1,1},{2,4},{3,5},{4,2},{5,3},{6,6},{7,7},{8,8},{9,9},{10,12... | collective-permute-start | bytes 1179656 | tf_op jit(solution)/shard_map/ppermute | solution.py:380
  97.7 26.5 %collective-permute-start.12 = (bf16[256,768]{1,0:T(8,128)(2,1)S(1)}, bf16[256,768]{1,0:T(8,128)(2,1)S(1)}, u32[]{:S(2)}, u32[]{:S(2)}) collective-permute-start(bf16[256,768]{1,0:T(8,128)(2,1)S(1)} %copy-done.30), channel_id=1, source_target_pairs={{0,1},{1,0},{2,5},{3,4},{4,3},{5,2},{6,7},{7,6},{8,9},{9,8},{10,13... | collective-permute-start | bytes 1179656 | tf_op jit(solution)/shard_map/ppermute | solution.py:381
  106.5 20.2 %collective-permute-start.9 = (bf16[768,384]{1,0:T(8,128)(2,1)S(1)}, bf16[768,384]{1,0:T(8,128)(2,1)S(1)}, u32[]{:S(2)}, u32[]{:S(2)}) collective-permute-start(bf16[768,384]{1,0:T(8,128)(2,1)S(1)} %slice.146), channel_id=1, source_target_pairs={{0,4},{4,0},{8,12},{12,8},{16,20},{20,16},{24,28},{28,24},{1,5},{5... | collective-permute-start | bytes 1769480 | tf_op jit(solution)/shard_map/ppermute | solution.py:394
  123.0 19.3 %collective-permute-start.18 = (bf16[384,768]{1,0:T(8,128)(2,1)}, bf16[384,768]{1,0:T(8,128)(2,1)}, u32[]{:S(2)}, u32[]{:S(2)}) collective-permute-start(bf16[384,768]{1,0:T(8,128)(2,1)} %all-gather.2.refs_5_), channel_id=1, source_target_pairs={{0,8},{4,12},{8,0},{12,4},{16,24},{20,28},{24,16},{28,20},{1,9},{5... | collective-permute-start | bytes 1769480 | tf_op jit(solution)/shard_map/ppermute | solution.py:397
  126.7 24.5 %collective-permute-start.13 = (bf16[512,768]{1,0:T(8,128)(2,1)}, bf16[512,768]{1,0:T(8,128)(2,1)}, u32[]{:S(2)}, u32[]{:S(2)}) collective-permute-start(bf16[512,768]{1,0:T(8,128)(2,1)} %pad_maximum_fusion.2.refs_2_), channel_id=1, source_target_pairs={{0,4},{4,0},{8,12},{12,8},{16,20},{20,16},{24,28},{28,24},{1,5},{5... | collective-permute-start | bytes 2359304 | tf_op jit(solution)/shard_map/ppermute | solution.py:394
  129.9 21.6 %collective-permute-start.10 = (bf16[512,768]{1,0:T(8,128)(2,1)}, bf16[512,768]{1,0:T(8,128)(2,1)}, u32[]{:S(2)}, u32[]{:S(2)}) collective-permute-start(bf16[512,768]{1,0:T(8,128)(2,1)} %add_convert_fusion.2.refs_0_), channel_id=1, source_target_pairs={{0,4},{4,0},{8,12},{12,8},{16,20},{20,16},{24,28},{28,24},{1,5},{5... | collective-permute-start | bytes 2359304 | tf_op jit(solution)/shard_map/ppermute | solution.py:394
  139.4 31.5 %collective-permute-start.15 = (bf16[384,384]{1,0:T(8,128)(2,1)}, bf16[384,384]{1,0:T(8,128)(2,1)}, u32[]{:S(2)}, u32[]{:S(2)}) collective-permute-start(bf16[384,384]{1,0:T(8,128)(2,1)} %slice.150), channel_id=1, source_target_pairs={{0,16},{4,20},{8,24},{12,28},{16,0},{20,4},{24,8},{28,12},{1,17},{... | collective-permute-start | bytes 884744 | tf_op jit(solution)/shard_map/ppermute | solution.py:400
  142.3 28.6 %collective-permute-start.17 = (bf16[384,384]{1,0:T(8,128)(2,1)}, bf16[384,384]{1,0:T(8,128)(2,1)}, u32[]{:S(2)}, u32[]{:S(2)}) collective-permute-start(bf16[384,384]{1,0:T(8,128)(2,1)} %slice.151), channel_id=1, source_target_pairs={{0,8},{4,12},{8,0},{12,4},{16,24},{20,28},{24,16},{28,20},{1,9},{5... | collective-permute-start | bytes 884744 | tf_op jit(solution)/shard_map/ppermute | solution.py:397
  146.2 24.7 %collective-permute-start.19 = (bf16[192,768]{1,0:T(8,128)(2,1)}, bf16[192,768]{1,0:T(8,128)(2,1)}, u32[]{:S(2)}, u32[]{:S(2)}) collective-permute-start(bf16[192,768]{1,0:T(8,128)(2,1)} %slice.152), channel_id=1, source_target_pairs={{0,16},{4,20},{8,24},{12,28},{16,0},{20,4},{24,8},{28,12},{1,17},{... | collective-permute-start | bytes 884744 | tf_op jit(solution)/shard_map/ppermute | solution.py:400
  151.2 19.7 %collective-permute-start.21 = (bf16[192,768]{1,0:T(8,128)(2,1)}, bf16[192,768]{1,0:T(8,128)(2,1)S(1)}, u32[]{:S(2)}, u32[]{:S(2)}) collective-permute-start(bf16[192,768]{1,0:T(8,128)(2,1)} %slice.153), channel_id=1, source_target_pairs={{0,8},{4,12},{8,0},{12,4},{16,24},{20,28},{24,16},{28,20},{1,9},{5... | collective-permute-start | bytes 884744 | tf_op jit(solution)/shard_map/ppermute | solution.py:397
  184.4 75.1 %collective-permute-start.25 = (f32[512,768]{1,0:T(8,128)}, f32[512,768]{1,0:T(8,128)}, u32[]{:S(2)}, u32[]{:S(2)}) collective-permute-start(f32[512,768]{1,0:T(8,128)} %get-tuple-element.58), channel_id=1, source_target_pairs={{0,4},{4,0},{8,12},{12,8},{16,20},{20,16},{24,28},{28,24},{1,5},{5... | collective-permute-start | bytes 4718600 | tf_op jit(solution)/shard_map/ppermute | solution.py:394
  187.9 22.8 %collective-permute-start.49 = (bf16[384,384]{1,0:T(8,128)(2,1)}, bf16[384,384]{1,0:T(8,128)(2,1)S(1)}, u32[]{:S(2)}, u32[]{:S(2)}) collective-permute-start(bf16[384,384]{1,0:T(8,128)(2,1)} %get-tuple-element.74), channel_id=1, source_target_pairs={{0,16},{4,20},{8,24},{12,28},{16,0},{20,4},{24,8},{28,12},{1,17},{... | collective-permute-start | bytes 884744 | tf_op jit(solution)/shard_map/ppermute | solution.py:400
  189.4 27.6 %collective-permute-start.44 = (bf16[384,384]{1,0:T(8,128)(2,1)}, bf16[384,384]{1,0:T(8,128)(2,1)S(1)}, u32[]{:S(2)}, u32[]{:S(2)}) collective-permute-start(bf16[384,384]{1,0:T(8,128)(2,1)} %get-tuple-element.68), channel_id=1, source_target_pairs={{0,8},{4,12},{8,0},{12,4},{16,24},{20,28},{24,16},{28,20},{1,9},{5... | collective-permute-start | bytes 884744 | tf_op jit(solution)/shard_map/ppermute | solution.py:397
  222.4 45.9 %collective-permute-start.22 = (f32[512,768]{1,0:T(8,128)S(1)}, f32[512,768]{1,0:T(8,128)S(1)}, u32[]{:S(2)}, u32[]{:S(2)}) collective-permute-start(f32[512,768]{1,0:T(8,128)S(1)} %copy-done.68), channel_id=1, source_target_pairs={{0,4},{4,0},{8,12},{12,8},{16,20},{20,16},{24,28},{28,24},{1,5},{5... | collective-permute-start | bytes 4718600 | tf_op jit(solution)/shard_map/ppermute | solution.py:394
  255.3 20.2 %collective-permute-start.66 = (bf16[96,768]{1,0:T(8,128)(2,1)S(1)}, bf16[96,768]{1,0:T(8,128)(2,1)S(1)}, u32[]{:S(2)}, u32[]{:S(2)}) collective-permute-start(bf16[96,768]{1,0:T(8,128)(2,1)S(1)} %fusion.42), channel_id=1, source_target_pairs={{0,24},{4,28},{8,16},{12,20},{16,8},{20,12},{24,0},{28,4},{1,25},{... | collective-permute-start | bytes 442376 | tf_op jit(solution)/shard_map/ppermute | solution.py:460
  256.6 18.9 %collective-permute-start.67 = (bf16[96,768]{1,0:T(8,128)(2,1)S(1)}, bf16[96,768]{1,0:T(8,128)(2,1)S(1)}, u32[]{:S(2)}, u32[]{:S(2)}) collective-permute-start(bf16[96,768]{1,0:T(8,128)(2,1)S(1)} %fusion.42), channel_id=1, source_target_pairs={{0,16},{4,20},{8,24},{12,28},{16,0},{20,4},{24,8},{28,12},{1,17},{... | collective-permute-start | bytes 442376 | tf_op jit(solution)/shard_map/ppermute | solution.py:400
  257.8 17.8 %collective-permute-start.68 = (bf16[96,768]{1,0:T(8,128)(2,1)S(1)}, bf16[96,768]{1,0:T(8,128)(2,1)S(1)}, u32[]{:S(2)}, u32[]{:S(2)}) collective-permute-start(bf16[96,768]{1,0:T(8,128)(2,1)S(1)} %fusion.42), channel_id=1, source_target_pairs={{0,8},{4,12},{8,0},{12,4},{16,24},{20,28},{24,16},{28,20},{1,9},{5... | collective-permute-start | bytes 442376 | tf_op jit(solution)/shard_map/ppermute | solution.py:397
  259.5 17.7 %collective-permute-start.56 = (bf16[4,192,384]{2,1,0:T(8,128)(2,1)S(1)}, bf16[4,192,384]{2,1,0:T(8,128)(2,1)S(1)}, u32[]{:S(2)}, u32[]{:S(2)}) collective-permute-start(bf16[4,192,384]{2,1,0:T(8,128)(2,1)S(1)} %get-tuple-element.176), channel_id=1, source_target_pairs={{0,4},{4,0},{8,12},{12,8},{16,20},{20,16},{24,28},{28,24},{1,5},{5... | collective-permute-start | bytes 1769480 | tf_op jit(solution)/shard_map/ppermute | solution.py:394
  276.7 54.5 %collective-permute-start.69 = (bf16[4,96,768]{2,1,0:T(8,128)(2,1)}, bf16[4,96,768]{2,1,0:T(8,128)(2,1)}, u32[]{:S(2)}, u32[]{:S(2)}) collective-permute-start(bf16[4,96,768]{2,1,0:T(8,128)(2,1)} %get-tuple-element.167), channel_id=1, source_target_pairs={{0,4},{4,0},{8,12},{12,8},{16,20},{20,16},{24,28},{28,24},{1,5},{5... | collective-permute-start | bytes 1769480 | tf_op jit(solution)/shard_map/ppermute | solution.py:394
  350.7 46.7 %collective-permute-start.23 = (bf16[256,768]{1,0:T(8,128)(2,1)S(1)}, bf16[256,768]{1,0:T(8,128)(2,1)S(1)}, u32[]{:S(2)}, u32[]{:S(2)}) collective-permute-start(bf16[256,768]{1,0:T(8,128)(2,1)S(1)} %get-tuple-element.145), channel_id=1, source_target_pairs={{0,0},{1,1},{4,2},{5,3},{2,4},{3,5},{6,6},{7,7},{8,8},{9,9},{12,10... | collective-permute-start | bytes 1179656 | tf_op jit(solution)/shard_map/ppermute | solution.py:389
  355.2 42.2 %collective-permute-start.24 = (bf16[256,768]{1,0:T(8,128)(2,1)S(1)}, bf16[256,768]{1,0:T(8,128)(2,1)S(1)}, u32[]{:S(2)}, u32[]{:S(2)}) collective-permute-start(bf16[256,768]{1,0:T(8,128)(2,1)S(1)} %get-tuple-element.146), channel_id=1, source_target_pairs={{1,0},{0,1},{5,2},{4,3},{3,4},{2,5},{7,6},{6,7},{9,8},{8,9},{13,10... | collective-permute-start | bytes 1179656 | tf_op jit(solution)/shard_map/ppermute | solution.py:390
  358.0 26.6 %collective-permute-start.38 = (bf16[48,1664]{1,0:T(8,128)(2,1)S(1)}, bf16[48,1664]{1,0:T(8,128)(2,1)S(1)}, u32[]{:S(2)}, u32[]{:S(2)}) collective-permute-start(bf16[48,1664]{1,0:T(8,128)(2,1)S(1)} %get-tuple-element.164), channel_id=1, source_target_pairs={{0,2},{1,3},{2,0},{3,1},{4,6},{5,7},{6,4},{7,5},{8,10},{9,11},{10,... | collective-permute-start | bytes 479240 | tf_op jit(solution)/shard_map/ppermute | solution.py:453
  359.2 27.1 %collective-permute-start.37 = (bf16[48,1664]{1,0:T(8,128)(2,1)S(1)}, bf16[48,1664]{1,0:T(8,128)(2,1)S(1)}, u32[]{:S(2)}, u32[]{:S(2)}) collective-permute-start(bf16[48,1664]{1,0:T(8,128)(2,1)S(1)} %get-tuple-element.163), channel_id=1, source_target_pairs={{0,1},{1,2},{2,3},{3,0},{4,5},{5,6},{6,7},{7,4},{8,9},{9,10},{10,1... | collective-permute-start | bytes 479240 | tf_op jit(solution)/shard_map/ppermute | solution.py:453
  396.6 18.1 %collective-permute-start.29 = (bf16[256,768]{1,0:T(8,128)(2,1)S(1)}, bf16[256,768]{1,0:T(8,128)(2,1)S(1)}, u32[]{:S(2)}, u32[]{:S(2)}) collective-permute-start(bf16[256,768]{1,0:T(8,128)(2,1)S(1)} %get-tuple-element.140), channel_id=1, source_target_pairs={{1,0},{0,1},{5,2},{4,3},{3,4},{2,5},{7,6},{6,7},{9,8},{8,9},{13,10... | collective-permute-start | bytes 1179656 | tf_op jit(solution)/shard_map/ppermute | solution.py:390
  397.3 18.5 %collective-permute-start.43 = (bf16[4,48,1664]{2,1,0:T(8,128)(2,1)S(1)}, bf16[4,48,1664]{2,1,0:T(8,128)(2,1)S(1)}, u32[]{:S(2)}, u32[]{:S(2)}) collective-permute-start(bf16[4,48,1664]{2,1,0:T(8,128)(2,1)S(1)} %get-tuple-element.158), channel_id=1, source_target_pairs={{0,4},{4,0},{8,12},{12,8},{16,20},{20,16},{24,28},{28,24},{1,5},{5... | collective-permute-start | bytes 1916936 | tf_op jit(solution)/shard_map/ppermute | solution.py:394
  (114 other events, 1149.5 us)
